TPU v7x, 32 devices: a whole 2x2x4 slice. The times are simulated.
32 devices in a mesh: dp: 16 (over z, y, x), shard: 2 (over core).
Axes of the slice: x: 2, y: 2, z: 4, core: 2. Of those that a mesh axis runs over, the one named last changes fastest.
Arguments:
- tokens: bfloat16 [16, 1024, 512], P('dp', 'shard'), may hold values from -6 to 6
- segments: int32 [16, 1024], P('dp'), may hold values from 0 to 6, as said below
- fill_length: int32 [16], P('dp'), may hold values from 640 to 1024
- query_weight: bfloat16 [512, 512], P(('dp', 'shard')), may hold values from -0.375 to 0.375
- key_weight: bfloat16 [512, 512], P(('dp', 'shard')), may hold values from -0.375 to 0.375
- value_weight: bfloat16 [512, 512], P(('dp', 'shard')), may hold values from -0.25 to 0.25
- output_weight: bfloat16 [512, 512], P(('dp', 'shard')), may hold values from -1.5 to 1.5
- query_bias: bfloat16 [512], P(('dp', 'shard')), may hold values from -4 to 4
- value_bias: bfloat16 [512], P(('dp', 'shard')), may hold values from -4 to 4
- output_bias: bfloat16 [512], P(('dp', 'shard')), may hold values from -6 to 6
- inner_weight: bfloat16 [512, 2048], P(('dp', 'shard')), may hold values from -0.25 to 0.25
- inner_bias: bfloat16 [2048], P(('dp', 'shard')), may hold values from -6 to 6
- outer_weight: bfloat16 [2048, 512], P(('dp', 'shard')), may hold values from -0.125 to 0.125
- outer_bias: bfloat16 [512], P(('dp', 'shard')), may hold values from -6 to 6
- residual_gates: float32 [2], replicated, may hold values from 0.5 to 1.5
- cotangent: bfloat16 [16, 1024, 512], P('dp', 'shard'), may hold values from -6 to 6
Outputs:
- layer_output: bfloat16 [16, 1024, 512], P('dp', 'shard')
- token_grads: float32 [16, 1024, 512], P('dp', 'shard')
- grad_query_weight: float32 [512, 512], P(('dp', 'shard'))
- grad_key_weight: float32 [512, 512], P(('dp', 'shard'))
- grad_value_weight: float32 [512, 512], P(('dp', 'shard'))
- grad_output_weight: float32 [512, 512], P(('dp', 'shard'))
- grad_query_bias: float32 [512], P(('dp', 'shard'))
- grad_value_bias: float32 [512], P(('dp', 'shard'))
- grad_output_bias: float32 [512], P(('dp', 'shard'))
- grad_inner_weight: float32 [512, 2048], P(('dp', 'shard'))
- grad_inner_bias: float32 [2048], P(('dp', 'shard'))
- grad_outer_weight: float32 [2048, 512], P(('dp', 'shard'))
- grad_outer_bias: float32 [512], P(('dp', 'shard'))
- grad_residual_gates: float32 [2], replicated
Inputs may be any that keep to these rules, and one draw needn't show every extreme that they name: `segments`: numbers never fall along a row; positions with one number form one packed sentence pair.
All inputs are finite; a program needn't handle non-finite values.
Results may differ from a plain program's by a relative error of at most 0.012.
The roundings to bfloat16 on the way count: a program that leaves them out, or rounds other values in their place, can miss the bound.
Values may be sent and summed in bfloat16 or wider, within the bound.
A program may use at most 128 MiB of HBM per device.

v0:
```python
import jax
import jax.numpy as jnp
from jax import lax
from jax.sharding import PartitionSpec as P

HEADS = 8


def exact_gelu(value):
    return jax.nn.gelu(value, approximate=False)


def allowed_mask(seg_queries, places, seg_keys, fill_row):
    key_places = jnp.arange(seg_keys.shape[0], dtype=jnp.int32)
    same = seg_queries[:, None] == seg_keys[None, :]
    live = (key_places[None, :] < fill_row) | (key_places[None, :] == places[:, None])
    return same & live


def head_forward(queries, keys_all, values_all, allowed, score_scale):
    scores = (
        jnp.einsum("qd,kd->qk", queries, keys_all, preferred_element_type=jnp.float32) * score_scale
    )
    scores = jnp.where(allowed, scores, -1e30)
    highest = jnp.max(scores, axis=-1, keepdims=True)
    expo = jnp.exp(scores - highest)
    totals = jnp.sum(expo, axis=-1, keepdims=True)
    weights_low = (expo / totals).astype(jnp.bfloat16)
    attended = jnp.einsum(
        "qk,kd->qd", weights_low, values_all, preferred_element_type=jnp.float32
    ).astype(jnp.bfloat16)
    return (attended, (highest + jnp.log(totals))[:, 0])


def head_backward(queries, keys_all, values_all, allowed, score_scale, logsum, grad_attended):
    scores = (
        jnp.einsum("qd,kd->qk", queries, keys_all, preferred_element_type=jnp.float32) * score_scale
    )
    scores = jnp.where(allowed, scores, -1e30)
    weights = jnp.exp(scores - logsum[:, None])
    grad_weights = jnp.einsum(
        "qd,kd->qk", grad_attended, values_all, preferred_element_type=jnp.float32
    )
    grad_values = jnp.einsum(
        "qk,qd->kd", weights.astype(jnp.bfloat16), grad_attended, preferred_element_type=jnp.float32
    )
    inner = jnp.sum(weights * grad_weights, axis=-1, keepdims=True)
    grad_scores = (weights * (grad_weights - inner)).astype(jnp.bfloat16)
    grad_queries = (
        jnp.einsum("qk,kd->qd", grad_scores, keys_all, preferred_element_type=jnp.float32)
        * score_scale
    )
    grad_keys = (
        jnp.einsum("qk,qd->kd", grad_scores, queries, preferred_element_type=jnp.float32)
        * score_scale
    )
    return (grad_queries, grad_keys, grad_values)


def attend_rows(
    queries, keys_all, values_all, seg_queries, places, seg_keys, fill_rows, score_scale
):

    def per_row(row_items):
        row_queries, row_keys, row_values, row_segq, row_segk, row_fill = row_items
        allowed = allowed_mask(row_segq, places, row_segk, row_fill)

        def per_head(head_parts):
            return head_forward(head_parts[0], head_parts[1], head_parts[2], allowed, score_scale)

        attended, logsum = lax.map(
            per_head,
            (
                jnp.swapaxes(row_queries, 0, 1),
                jnp.swapaxes(row_keys, 0, 1),
                jnp.swapaxes(row_values, 0, 1),
            ),
        )
        return (jnp.swapaxes(attended, 0, 1), logsum)

    return lax.map(per_row, (queries, keys_all, values_all, seg_queries, seg_keys, fill_rows))


def attend_back(
    queries,
    keys_all,
    values_all,
    seg_queries,
    places,
    seg_keys,
    fill_rows,
    score_scale,
    logsum,
    grad_attended,
):

    def per_row(row_items):
        row_queries, row_keys, row_values, row_segq, row_segk, row_fill, row_logsum, row_grad = (
            row_items
        )
        allowed = allowed_mask(row_segq, places, row_segk, row_fill)

        def per_head(head_parts):
            return head_backward(
                head_parts[0],
                head_parts[1],
                head_parts[2],
                allowed,
                score_scale,
                head_parts[3],
                head_parts[4],
            )

        grad_queries, grad_keys, grad_values = lax.map(
            per_head,
            (
                jnp.swapaxes(row_queries, 0, 1),
                jnp.swapaxes(row_keys, 0, 1),
                jnp.swapaxes(row_values, 0, 1),
                row_logsum,
                jnp.swapaxes(row_grad, 0, 1),
            ),
        )
        return (
            jnp.swapaxes(grad_queries, 0, 1),
            jnp.swapaxes(grad_keys, 0, 1),
            jnp.swapaxes(grad_values, 0, 1),
        )

    return lax.map(
        per_row,
        (queries, keys_all, values_all, seg_queries, seg_keys, fill_rows, logsum, grad_attended),
    )


def on_device(
    tokens,
    segments,
    fill_length,
    query_weight,
    key_weight,
    value_weight,
    output_weight,
    query_bias,
    value_bias,
    output_bias,
    inner_weight,
    inner_bias,
    outer_weight,
    outer_bias,
    residual_gates,
    cotangent,
):
    row_count, half_len, width = tokens.shape
    head_depth = width // HEADS
    score_scale = head_depth ** (-0.5)
    token_rows = row_count * half_len
    source = tokens.reshape(token_rows, width)
    seq_len = half_len * lax.axis_size("shard")
    query_full, key_full, value_full, output_full, bias_query, bias_value, bias_output = (
        lax.all_gather(query_weight, ("dp", "shard"), axis=0, tiled=True),
        lax.all_gather(key_weight, ("dp", "shard"), axis=0, tiled=True),
        lax.all_gather(value_weight, ("dp", "shard"), axis=0, tiled=True),
        lax.all_gather(output_weight, ("dp", "shard"), axis=0, tiled=True),
        lax.all_gather(query_bias, ("dp", "shard"), axis=0, tiled=True),
        lax.all_gather(value_bias, ("dp", "shard"), axis=0, tiled=True),
        lax.all_gather(output_bias, ("dp", "shard"), axis=0, tiled=True),
    )
    head_shape = (row_count, half_len, HEADS, head_depth)
    queries = (
        (jnp.dot(source, query_full, preferred_element_type=jnp.float32) + bias_query)
        .astype(jnp.bfloat16)
        .reshape(head_shape)
    )
    keys_local = (
        jnp.dot(source, key_full, preferred_element_type=jnp.float32)
        .astype(jnp.bfloat16)
        .reshape(head_shape)
    )
    values_local = (
        (jnp.dot(source, value_full, preferred_element_type=jnp.float32) + bias_value)
        .astype(jnp.bfloat16)
        .reshape(head_shape)
    )
    head_queries, head_keys, head_values = (
        lax.all_to_all(queries, "shard", split_axis=2, concat_axis=1, tiled=True),
        lax.all_to_all(keys_local, "shard", split_axis=2, concat_axis=1, tiled=True),
        lax.all_to_all(values_local, "shard", split_axis=2, concat_axis=1, tiled=True),
    )
    places = jnp.arange(seq_len, dtype=jnp.int32)
    attended_heads, logsum = attend_rows(
        head_queries, head_keys, head_values, segments, places, segments, fill_length, score_scale
    )
    attended = lax.all_to_all(attended_heads, "shard", split_axis=1, concat_axis=2, tiled=True)
    attended_rows = attended.reshape(token_rows, width)
    attn = jnp.dot(attended_rows, output_full, preferred_element_type=jnp.float32) + bias_output
    gate_attn = residual_gates[0]
    gate_feed = residual_gates[1]
    resid = source.astype(jnp.float32) + gate_attn * attn
    resid_low = resid.astype(jnp.bfloat16)
    inner_full, bias_inner, outer_full, bias_outer = (
        lax.all_gather(inner_weight, ("dp", "shard"), axis=0, tiled=True),
        lax.all_gather(inner_bias, ("dp", "shard"), axis=0, tiled=True),
        lax.all_gather(outer_weight, ("dp", "shard"), axis=0, tiled=True),
        lax.all_gather(outer_bias, ("dp", "shard"), axis=0, tiled=True),
    )
    hidden = jnp.dot(resid_low, inner_full, preferred_element_type=jnp.float32) + bias_inner
    activ, gelu_back = jax.vjp(exact_gelu, hidden)
    activ_low = activ.astype(jnp.bfloat16)
    ffn = jnp.dot(activ_low, outer_full, preferred_element_type=jnp.float32) + bias_outer
    layer = (resid + gate_feed * ffn).astype(jnp.bfloat16).reshape(row_count, half_len, width)
    upstream = cotangent.reshape(token_rows, width).astype(jnp.float32)
    gate_feed_part = jnp.sum(upstream * ffn)
    grad_ffn = (gate_feed * upstream).astype(jnp.bfloat16)
    inner_back, outer_back = (
        lax.all_gather(inner_weight, ("dp", "shard"), axis=0, tiled=True),
        lax.all_gather(outer_weight, ("dp", "shard"), axis=0, tiled=True),
    )
    grad_outer_w = jnp.einsum("tf,td->fd", activ_low, grad_ffn, preferred_element_type=jnp.float32)
    grad_outer_b = jnp.sum(grad_ffn.astype(jnp.float32), axis=0)
    grad_activ = jnp.einsum("td,fd->tf", grad_ffn, outer_back, preferred_element_type=jnp.float32)
    grad_hidden = gelu_back(grad_activ)[0].astype(jnp.bfloat16)
    grad_inner_w = jnp.einsum(
        "td,tf->df", resid_low, grad_hidden, preferred_element_type=jnp.float32
    )
    grad_inner_b = jnp.sum(grad_hidden.astype(jnp.float32), axis=0)
    grad_resid = upstream + jnp.einsum(
        "tf,df->td", grad_hidden, inner_back, preferred_element_type=jnp.float32
    )
    inner_sum, inner_bsum, outer_sum, outer_bsum = (
        lax.psum_scatter(grad_inner_w, ("dp", "shard"), scatter_dimension=0, tiled=True),
        lax.psum_scatter(grad_inner_b, ("dp", "shard"), scatter_dimension=0, tiled=True),
        lax.psum_scatter(grad_outer_w, ("dp", "shard"), scatter_dimension=0, tiled=True),
        lax.psum_scatter(grad_outer_b, ("dp", "shard"), scatter_dimension=0, tiled=True),
    )
    gate_attn_part = jnp.sum(grad_resid * attn)
    grad_attn = (gate_attn * grad_resid).astype(jnp.bfloat16)
    query_back, key_back, value_back, output_back = (
        lax.all_gather(query_weight, ("dp", "shard"), axis=0, tiled=True),
        lax.all_gather(key_weight, ("dp", "shard"), axis=0, tiled=True),
        lax.all_gather(value_weight, ("dp", "shard"), axis=0, tiled=True),
        lax.all_gather(output_weight, ("dp", "shard"), axis=0, tiled=True),
    )
    grad_output_w = jnp.einsum(
        "td,te->de", attended_rows, grad_attn, preferred_element_type=jnp.float32
    )
    grad_output_b = jnp.sum(grad_attn.astype(jnp.float32), axis=0)
    grad_attended = (
        jnp.einsum("te,de->td", grad_attn, output_back, preferred_element_type=jnp.float32)
        .astype(jnp.bfloat16)
        .reshape(head_shape)
    )
    grad_attended_heads = lax.all_to_all(
        grad_attended, "shard", split_axis=2, concat_axis=1, tiled=True
    )
    head_gq, head_gk, head_gv = attend_back(
        head_queries,
        head_keys,
        head_values,
        segments,
        places,
        segments,
        fill_length,
        score_scale,
        logsum,
        grad_attended_heads,
    )
    grad_queries, grad_keys, grad_values = (
        lax.all_to_all(
            head_gq.astype(jnp.bfloat16), "shard", split_axis=1, concat_axis=2, tiled=True
        ),
        lax.all_to_all(
            head_gk.astype(jnp.bfloat16), "shard", split_axis=1, concat_axis=2, tiled=True
        ),
        lax.all_to_all(
            head_gv.astype(jnp.bfloat16), "shard", split_axis=1, concat_axis=2, tiled=True
        ),
    )
    grad_queries = grad_queries.reshape(token_rows, width)
    grad_keys = grad_keys.reshape(token_rows, width)
    grad_values = grad_values.reshape(token_rows, width)
    grad_query_w = jnp.einsum("td,te->de", source, grad_queries, preferred_element_type=jnp.float32)
    grad_key_w = jnp.einsum("td,te->de", source, grad_keys, preferred_element_type=jnp.float32)
    grad_value_w = jnp.einsum("td,te->de", source, grad_values, preferred_element_type=jnp.float32)
    grad_query_b = jnp.sum(grad_queries.astype(jnp.float32), axis=0)
    grad_value_b = jnp.sum(grad_values.astype(jnp.float32), axis=0)
    grad_source = grad_resid + jnp.einsum(
        "te,de->td", grad_queries, query_back, preferred_element_type=jnp.float32
    )
    grad_source = grad_source + jnp.einsum(
        "te,de->td", grad_keys, key_back, preferred_element_type=jnp.float32
    )
    grad_source = grad_source + jnp.einsum(
        "te,de->td", grad_values, value_back, preferred_element_type=jnp.float32
    )
    device_count = lax.axis_size(("dp", "shard"))
    gate_term = jnp.broadcast_to(
        jnp.stack([gate_attn_part, gate_feed_part])[None, :], (device_count, 2)
    )
    query_sum, key_sum, value_sum, output_sum, qbias_sum, vbias_sum, obias_sum, gate_sum = (
        lax.psum_scatter(grad_query_w, ("dp", "shard"), scatter_dimension=0, tiled=True),
        lax.psum_scatter(grad_key_w, ("dp", "shard"), scatter_dimension=0, tiled=True),
        lax.psum_scatter(grad_value_w, ("dp", "shard"), scatter_dimension=0, tiled=True),
        lax.psum_scatter(grad_output_w, ("dp", "shard"), scatter_dimension=0, tiled=True),
        lax.psum_scatter(grad_query_b, ("dp", "shard"), scatter_dimension=0, tiled=True),
        lax.psum_scatter(grad_value_b, ("dp", "shard"), scatter_dimension=0, tiled=True),
        lax.psum_scatter(grad_output_b, ("dp", "shard"), scatter_dimension=0, tiled=True),
        lax.psum_scatter(gate_term, ("dp", "shard"), scatter_dimension=0, tiled=True),
    )
    return (
        layer,
        grad_source.reshape(row_count, half_len, width),
        query_sum,
        key_sum,
        value_sum,
        output_sum,
        qbias_sum,
        vbias_sum,
        obias_sum,
        inner_sum,
        inner_bsum,
        outer_sum,
        outer_bsum,
        gate_sum.reshape(2),
    )


def solution(mesh):
    return jax.shard_map(
        on_device,
        mesh=mesh,
        in_specs=(
            P("dp", "shard", None),
            P("dp", None),
            P("dp"),
            P(("dp", "shard"), None),
            P(("dp", "shard"), None),
            P(("dp", "shard"), None),
            P(("dp", "shard"), None),
            P(("dp", "shard")),
            P(("dp", "shard")),
            P(("dp", "shard")),
            P(("dp", "shard"), None),
            P(("dp", "shard")),
            P(("dp", "shard"), None),
            P(("dp", "shard")),
            P(),
            P("dp", "shard", None),
        ),
        out_specs=(
            P("dp", "shard", None),
            P("dp", "shard", None),
            P(("dp", "shard"), None),
            P(("dp", "shard"), None),
            P(("dp", "shard"), None),
            P(("dp", "shard"), None),
            P(("dp", "shard")),
            P(("dp", "shard")),
            P(("dp", "shard")),
            P(("dp", "shard"), None),
            P(("dp", "shard")),
            P(("dp", "shard"), None),
            P(("dp", "shard")),
            P(),
        ),
        check_vma=False,
    )
```

profile of v0, /device:TPU:0, one launch (start us, length us, event | category | flops | bytes accessed | tf_op | source)
XLA Modules:
  0.0 1176.8 jit_solution(7081747435970034667)
XLA Ops:
  12.2 42.1 %all-reduce.12 = (bf16[512]{0:T(512)(128)(2,1)S(1)}, bf16[512]{0:T(512)(128)(2,1)S(1)}, bf16[512]{0:T(512)(128)(2,1)S(1)}, bf16[2048]{0:T(1024)(128)(2,1)S(1)}, bf16[512]{0:T(512)(128)(2,1)S(1)}) all-reduce(bf16[512]{0:T(512)(128)(2,1)S(1)} %dynamic-update-slice, ...), channel_id=1, replica_groups=mesh['dp'=16,'shard'=2] {'dp','shard'}, use_global_device_ids=true, to_apply=%add | all-reduce | flops 4096 | bytes 16384
  54.3 42.1 %all_gather.39 = bf16[512,512]{1,0:T(8,128)(2,1)S(1)} all-gather(bf16[16,512]{1,0:T(8,128)(2,1)} %param.23), channel_id=1, replica_groups=mesh['dp'=16,'shard'=2] {'dp','shard'}, dimensions={0}, use_global_device_ids=true | all-gather | bytes 540672 | tf_op jit(solution)/shard_map/all_gather | solution.py:161
  96.4 2.5 fusion.60
  98.9 3.5 all-to-all-start
  103.2 38.7 %all_gather.41 = bf16[512,512]{1,0:T(8,128)(2,1)S(1)} all-gather(bf16[16,512]{1,0:T(8,128)(2,1)} %param.24), channel_id=1, replica_groups=mesh['dp'=16,'shard'=2] {'dp','shard'}, dimensions={0}, use_global_device_ids=true | all-gather | bytes 540672 | tf_op jit(solution)/shard_map/all_gather | solution.py:162
  143.2 3.5 all-to-all-start.1
  147.2 39.9 %all_gather.42 = bf16[512,512]{1,0:T(8,128)(2,1)S(1)} all-gather(bf16[16,512]{1,0:T(8,128)(2,1)S(1)} %copy-done.26), channel_id=1, replica_groups=mesh['dp'=16,'shard'=2] {'dp','shard'}, dimensions={0}, use_global_device_ids=true | all-gather | bytes 540672 | tf_op jit(solution)/shard_map/all_gather | solution.py:163
  189.1 4.2 all-to-all-start.2
  195.2 2.4 copy.108
  198.2 17.5 %while.48 = (s32[]{:T(128)}, bf16[4,1024,64]{1,2,0:T(8,128)(2,1)}, f32[4,1024]{1,0:T(4,128)S(1)}, bf16[4,1024,64]{2,1,0:T(8,128)(2,1)S(1)}, bf16[4,1024,64]{2,1,...) while((s32[]{:T(128)}, bf16[4,1024,64]{1,2,0:T(8,128)(2,1)}, ...), condition=%wide.region_3.4_spmd.clone, body=%wide.region_0.3_spmd.clone.sunk | while | flops 281082880 | bytes 13552753 | solution.py:71
  200.1 2.5 fusion.132
  204.4 2.5 fusion.132
  208.8 2.5 fusion.132
  213.2 2.5 fusion.132
  215.8 2.5 copy.109
  218.3 2.6 bitcast_bitcast_fusion
  220.9 2.6 reshape.150
  223.5 3.5 all-to-all-start.3
  230.2 3.7 copy.128
  235.6 38.0 %all_gather.44 = bf16[512,512]{1,0:T(8,128)(2,1)S(1)} all-gather(bf16[16,512]{1,0:T(8,128)(2,1)S(1)} %copy-done.27), channel_id=1, replica_groups=mesh['dp'=16,'shard'=2] {'dp','shard'}, dimensions={0}, use_global_device_ids=true | all-gather | bytes 540672 | tf_op jit(solution)/shard_map/all_gather | solution.py:164
  273.6 2.1 fusion.64
  275.7 13.7 %multiply_convert_fusion.1 = (bf16[512,2048]{1,0:T(8,128)(2,1)}, f32[512,2048]{1,0:T(8,128)}, f32[512,2048]{1,0:T(8,128)}) fusion(f32[2048]{0:T(1024)S(1)} %convert_element_type.118, bf16[512,512]{1,0:T(8,128)(2,1)S(1)} %get-tuple-element.371, bf16[512,2048]{1,0:T(8,128)(2,1)} %all-gather.3.cloned.1.call-done), kind=kOutput, calls=%fused_computation.63 | convolution fusion | flops 1142947840 | bytes 13115392 | tf_op jit(solution)/shard_map/dot_general | solution.py:207
  289.4 7.4 convert_reduce_fusion
  300.6 4.3 multiply_reduce_fusion.1
  305.3 5.1 all_to_all.120
  312.0 32.7 %while.49 = (s32[]{:T(128)}, bf16[4,1024,64]{1,2,0:T(8,128)(2,1)}, bf16[4,1024,64]{1,2,0:T(8,128)(2,1)}, bf16[4,1024,64]{1,2,0:T(8,128)(2,1)}, bf16[4,1024,64]{2...) while((s32[]{:T(128)}, bf16[4,1024,64]{1,2,0:T(8,128)(2,1)}, ...), condition=%wide.region_6.7_spmd.clone, body=%wide.region_4.6_spmd.clone.sunk | while | flops 684850176 | bytes 48793924 | solution.py:114
  347.1 4.2 all_to_all.121
  354.5 2.5 copy.132
  358.5 1.9 reshape.154
  360.4 4.2 all_to_all.122
  366.1 2.7 copy.130
  370.3 2.6 copy.134
  372.9 2.3 copy.120
  375.2 1.9 reshape.156
  377.1 4.9 all_to_all.123
  382.0 2.5 reshape.157
  384.6 2.7 copy.131
  389.6 2.6 copy.136
  392.3 2.5 fusion.81
  395.1 4.8 fusion.82
  400.0 5.5 fusion.72
  408.3 37.5 %all-reduce.11 = (f32[512]{0:T(512)S(1)}, f32[512]{0:T(512)S(1)}, f32[512]{0:T(512)S(1)}, f32[2048]{0:T(1024)S(1)}, f32[512]{0:T(512)S(1)}, /*index=5*/f32[32,2]{1,0:T(8,128)S(1)}) all-reduce(f32[512]{0:T(512)S(1)} %reduce_sum.86, f32[512]{0:T(512)S(1)} %reduce_sum.88, ...), channel_id=6, replica_groups=mesh['dp'=16,'shard'=2] {'dp','shard'}, use_global_device_ids=true, to_apply=%region_12.13.clone | all-reduce | flops 4160 | bytes 33280
  453.1 36.8 %reduce-scatter.19.cloned.1.call-done = f32[16,512]{1,0:T(8,128)} async-done(((f32[512,512]{1,0:T(8,128)}), f32[16,512]{1,0:T(8,128)}) %reduce-scatter.19.cloned.1.call-update) | async-done | bytes 32784
  489.8 133.5 %reduce-scatter.21.cloned.1.call-done = f32[16,512]{1,0:T(8,128)} async-done(((f32[512,512]{1,0:T(8,128)}), f32[16,512]{1,0:T(8,128)}) %reduce-scatter.21.cloned.1.call-update) | async-done | bytes 32784
  623.3 133.4 %reduce-scatter.23.cloned.1.call-done = f32[16,512]{1,0:T(8,128)} async-done(((f32[512,512]{1,0:T(8,128)}), f32[16,512]{1,0:T(8,128)}) %reduce-scatter.23.cloned.1.call-update) | async-done | bytes 32784
  756.8 133.5 %reduce-scatter.13.cloned.1.call-done = f32[16,512]{1,0:T(8,128)} async-done(((f32[512,512]{1,0:T(8,128)}), f32[16,512]{1,0:T(8,128)}) %reduce-scatter.13.cloned.1.call-update) | async-done | bytes 32784 | tf_op jit(solution)/shard_map/reduce_scatter | solution.py:304
  890.2 139.7 %reduce-scatter.15.cloned.1.call-done = f32[16,2048]{1,0:T(8,128)} async-done(((f32[512,2048]{1,0:T(8,128)}), f32[16,2048]{1,0:T(8,128)}) %reduce-scatter.15.cloned.1.call-update) | async-done | bytes 131088 | tf_op jit(solution)/shard_map/reduce_scatter | solution.py:231
  1030.0 139.5 %reduce-scatter.17.cloned.1.call-done = f32[64,512]{1,0:T(8,128)} async-done(((f32[2048,512]{1,0:T(8,128)}), f32[64,512]{1,0:T(8,128)}) %reduce-scatter.17.cloned.1.call-update) | async-done | bytes 131088 | tf_op jit(solution)/shard_map/reduce_scatter | solution.py:233
  (232 shorter events, 84.5 us)
Async XLA Ops:
  7.2 134.7 %copy-start = (bf16[1,512,512]{2,1,0:T(8,128)(2,1)S(1)}, bf16[1,512,512]{2,1,0:T(8,128)(2,1)}, u32[]{:S(2)}) copy-start(bf16[1,512,512]{2,1,0:T(8,128)(2,1)} %param.20) | copy-start | bytes 1572868
  7.2 268.5 %all-gather.3.cloned.1.call-start = ((), (), s32[]{:S(2)}) async-start(), calls=%async_computation.14 | async-start | bytes 2162688 | tf_op jit(solution)/shard_map/all_gather | solution.py:202
  54.3 92.9 %copy-start.26 = (bf16[16,512]{1,0:T(8,128)(2,1)S(1)}, bf16[16,512]{1,0:T(8,128)(2,1)}, u32[]{:S(2)}) copy-start(bf16[16,512]{1,0:T(8,128)(2,1)} %param.25) | copy-start | bytes 49156
  96.4 6.8 copy-start.10
  98.9 44.3 %all-to-all-start = ((bf16[1,512,8,64]{1,3,0,2:T(8,128)(2,1)}), bf16[1,512,8,64]{1,3,0,2:T(8,128)(2,1)S(1)}, u32[]{:S(2)}, u32[]{:S(2)}) async-start(bf16[1,512,8,64]{1,3,0,2:T(8,128)(2,1)} %bitcast.3), calls=%async_computation | async-start | bytes 1048576 | tf_op jit(solution)/shard_map/all_to_all | solution.py:186
  102.4 187.0 %all-gather.5.cloned.1.call-start = ((), (), s32[]{:S(2)}) async-start(), calls=%async_computation.15 | async-start | bytes 2162688 | tf_op jit(solution)/shard_map/all_gather | solution.py:204
  141.9 4.8 copy-start.3
  143.2 45.9 %all-to-all-start.1 = ((bf16[1,512,8,64]{1,3,0,2:T(8,128)(2,1)}), bf16[1,512,8,64]{1,3,0,2:T(8,128)(2,1)S(1)}, u32[]{:S(2)}, u32[]{:S(2)}) async-start(bf16[1,512,8,64]{1,3,0,2:T(8,128)(2,1)} %bitcast.9), calls=%async_computation.1 | async-start | bytes 1048576 | tf_op jit(solution)/shard_map/all_to_all | solution.py:187
  146.7 51.5 %copy-start.31 = (s32[1,1024]{1,0:T(1,128)S(1)}, s32[1,1024]{1,0:T(1,128)}, u32[]{:S(2)}) copy-start(s32[1,1024]{1,0:T(1,128)} %param.21) | copy-start | bytes 12292
  189.1 6.1 all-to-all-start.2
  215.8 18.1 %copy-start.1 = (bf16[4,1024,64]{2,1,0:T(8,128)(2,1)}, bf16[4,1024,64]{2,1,0:T(8,128)(2,1)S(1)}, u32[]{:S(2)}) copy-start(bf16[4,1024,64]{2,1,0:T(8,128)(2,1)S(1)} %get-tuple-element.579) | copy-start | bytes 1572868
  218.3 16.7 %copy-start.28 = (f32[2]{0:T(128)S(1)}, f32[2]{0:T(128)}, u32[]{:S(2)}) copy-start(f32[2]{0:T(128)} %param.34) | copy-start | bytes 28
  218.3 17.3 %copy-start.27 = (bf16[16,512]{1,0:T(8,128)(2,1)S(1)}, bf16[16,512]{1,0:T(8,128)(2,1)}, u32[]{:S(2)}) copy-start(bf16[16,512]{1,0:T(8,128)(2,1)} %param.26) | copy-start | bytes 49156
  223.5 5.2 all-to-all-start.3
  226.9 262.9 %reduce-scatter.19.cloned.1.call-start = ((), (), s32[]{:S(2)}) async-start(), calls=%async_computation.19 | async-start | bytes 1081344
  275.7 13.7 %copy-start.13 = (bf16[512,512]{1,0:T(8,128)(2,1)}, bf16[512,512]{1,0:T(8,128)(2,1)S(1)}, u32[]{:S(2)}) copy-start(bf16[512,512]{1,0:T(8,128)(2,1)S(1)} %get-tuple-element.371) | copy-start | bytes 1572868
  289.4 7.5 copy-start.17
  289.4 7.5 copy-start.29
  296.9 8.0 copy-start.8
  296.9 2.4 copy-start.7
  296.9 3.0 copy-start.16
  296.9 3.7 copy-start.30
  298.2 6.6 copy-start.15
  304.8 5.6 copy-start.9
  312.0 1.8 copy-start.2
  315.6 1.2 copy-start.19
  316.7 1.8 copy-start.24
  317.3 2.1 copy-start.20
  320.1 1.8 copy-start.2
  324.9 1.8 copy-start.24
  325.4 2.1 copy-start.20
  328.3 1.8 copy-start.2
  333.1 1.8 copy-start.24
  333.6 2.1 copy-start.20
  336.5 1.8 copy-start.2
  341.2 1.8 copy-start.24
  341.8 2.1 copy-start.20
  352.0 5.1 copy-start.23
  357.0 266.3 %reduce-scatter.21.cloned.1.call-start = ((), (), s32[]{:S(2)}) async-start(), calls=%async_computation.20 | async-start | bytes 1081344
  372.9 383.9 %reduce-scatter.23.cloned.1.call-start = ((), (), s32[]{:S(2)}) async-start(), calls=%async_computation.21 | async-start | bytes 1081344
  389.6 5.5 copy-start.14
  392.2 498.0 %reduce-scatter.13.cloned.1.call-start = ((), (), s32[]{:S(2)}) async-start(), calls=%async_computation.16 | async-start | bytes 1081344 | tf_op jit(solution)/shard_map/reduce_scatter | solution.py:304
  394.7 5.2 copy-start.18
  394.8 635.2 %reduce-scatter.15.cloned.1.call-start = ((), (), s32[]{:S(2)}) async-start(), calls=%async_computation.17 | async-start | bytes 4325376 | tf_op jit(solution)/shard_map/reduce_scatter | solution.py:231
  399.9 769.6 %reduce-scatter.17.cloned.1.call-start = ((), (), s32[]{:S(2)}) async-start(), calls=%async_computation.18 | async-start | bytes 4325376 | tf_op jit(solution)/shard_map/reduce_scatter | solution.py:233
  405.5 45.6 %copy-start.4 = (bf16[512,512]{1,0:T(8,128)(2,1)S(1)}, bf16[512,512]{1,0:T(8,128)(2,1)}, u32[]{:S(2)}) copy-start(bf16[512,512]{1,0:T(8,128)(2,1)} %copy-done.3) | copy-start | bytes 1572868
  405.5 46.0 %copy-start.6 = (bf16[1,512,2,4,64]{1,4,3,2,0:T(8,128)(2,1)S(1)}, bf16[1,512,2,4,64]{1,4,3,2,0:T(8,128)(2,1)}, u32[]{:S(2)}) copy-start(bf16[1,512,2,4,64]{1,4,3,2,0:T(8,128)(2,1)} %copy-done.5) | copy-start | bytes 1572868
  445.7 5.8 copy-start.12
  (17 other events, 15.7 us)
Sparse Core Ops, SparseCore 0:
  10.9 60.2 all-gather.2
  106.1 53.7 all-gather.4
  357.1 132.6 reduce-scatter.18
  492.6 130.6 reduce-scatter.20
  626.0 130.7 reduce-scatter.22
  759.5 130.6 reduce-scatter.12
  893.1 136.8 reduce-scatter.14
  1032.8 136.6 reduce-scatter.16
where the time goes:
time: 1190 us; the launch traced here: 1180 us
  waiting for transfers between devices  721 us (61%)
  blocking collectives  257 us (22%)
  matrix products  92.4 us (8%)
  local copies, waits for them, and re-layouts  65.8 us (6%)
  between operations  15.8 us (1%)
  starting transfers between devices  15.3 us (1%)
    unnamed x11, waiting for transfers between devices  305 us
    reduce_scatter x1, waiting for transfers between devices, on_device(): lax.psum_scatter(grad_inner_w, ('dp', 'shard'), scatter_dimension=0, tile...  140 us
    reduce_scatter x1, waiting for transfers between devices, on_device(): lax.psum_scatter(grad_outer_w, ('dp', 'shard'), scatter_dimension=0, tile...  140 us
    reduce_scatter x1, waiting for transfers between devices, on_device(): lax.psum_scatter(grad_output_w, ('dp', 'shard'), scatter_dimension=0, til...  133 us
    unnamed x2, blocking collectives  79.6 us
    all_gather x1, blocking collectives, on_device(): lax.all_gather(query_weight, ('dp', 'shard'), axis=0, tiled=True)  42.1 us
    all_gather x1, blocking collectives, on_device(): lax.all_gather(value_weight, ('dp', 'shard'), axis=0, tiled=True)  39.9 us
    all_gather x1, blocking collectives, on_device(): lax.all_gather(key_weight, ('dp', 'shard'), axis=0, tiled=True)  38.7 us
  transfers between devices with their start and end apart: 12, of which 8 were waited for; matrix products, arithmetic and copies ran while one was open for 9% of the time, Pallas kernels for 0%

commit v1 on v0

v1 whole, which is shorter than its diff:
```python
import jax
import jax.numpy as jnp
from jax import lax
from jax.experimental import pallas as pl
from jax.experimental.pallas import tpu as pltpu
from jax.sharding import PartitionSpec as P

MESH = pl.DeviceIdType.MESH
BF = jnp.bfloat16
F32 = jnp.float32
HEADS = 8
GROUP = 16
PAIRS = 4
STEPS = 4


def dot(left, right, left_dim, right_dim):
    return lax.dot_general(
        left, right, (((left_dim,), (right_dim,)), ((), ())), preferred_element_type=F32
    )


def gelu_parts(hidden):
    size = jnp.abs(hidden) * 0.7071067811865476
    recip = 1.0 / (1.0 + 0.3275911 * size)
    expo = jnp.exp(-size * size)
    poly = recip * (
        0.127414796
        + recip * (-0.142248368 + recip * (0.7107068705 + recip * (-0.7265760135 + recip * 0.5307027145)))
    )
    tail = poly * expo
    cdf = jnp.where(hidden >= 0, 1.0 - tail, tail)
    return hidden * cdf, cdf + hidden * expo * 0.3989422804014327


def natural(value):
    width = value.shape[-1]
    return value.reshape(8, 4, 16, width).transpose(1, 0, 2, 3).reshape(512, width)


def by_chip(value):
    width = value.shape[-1]
    return value.reshape(4, 8, 16, width).transpose(1, 0, 2, 3).reshape(2, 2, 2, 64, width)


def col_sums(value):
    return dot(jnp.ones((8, value.shape[0]), BF), value, 1, 0)


def layer_kernel(
    tok,
    cot,
    seg,
    fill,
    gates,
    wcat,
    wout_proj,
    win,
    wout,
    layer_o,
    tg_o,
    gq_o,
    gk_o,
    gv_o,
    go_o,
    gi_o,
    gout_o,
    small_o,
    xrow,
    cotv,
    wq,
    wo,
    wf,
    maskb,
    qt,
    kt,
    vt,
    probs,
    st,
    pb,
    mixt,
    attn,
    rlow,
    gffn,
    gmixt,
    dqt,
    dkv,
    rkv,
    gf,
    rcf,
    s1f,
    r1f,
    s2f,
    r2f,
    s3f,
    r3f,
    s3o,
    r3o,
    go,
    rco,
    s1o,
    r1o,
    s2o,
    r2o,
    s3w,
    r3w,
    s1q,
    r1q,
    s2q,
    r2q,
    s3q,
    r3q,
    ksum,
    bb,
    rb,
    biasb,
    send_sem,
    recv_sem,
    local_sem,
):
    ffn, gres = maskb.at[pl.ds(0, 512)], maskb.at[pl.ds(512, 512)]
    hid, gac = st.at[pl.ds(0, 512)], st.at[pl.ds(512, 512)]
    act, ghid = pb.at[0, pl.ds(0, 512)], pb.at[0, pl.ds(512, 512)]

    dp = lax.axis_index("dp")
    c = lax.axis_index("shard")
    lo = lax.rem(dp, GROUP)
    z = lax.div(lo, 4)
    y = lax.rem(lax.div(lo, 2), 2)
    x = lax.rem(lo, 2)
    cc, xx, yy = 1 - c, 1 - x, 1 - y

    def zk(k):
        return lax.rem(z + (k % 4), 4)

    zs = [zk(k) for k in range(4)]
    XP = (dp + 1 - 2 * x, c)
    YP = (dp + 2 - 4 * y, c)
    ZP = [None] + [(dp + 4 * (zs[k] - z), c) for k in (1, 2, 3)]
    SB = (dp, cc)

    def rows(place):
        return pl.ds(pl.multiple_of(place * 16, 16), 16)

    def cols(place):
        return pl.ds(pl.multiple_of(place * 512, 512), 512)

    table = {}
    ids = {}

    def same(ref, dev):
        return (ref, ref, dev)

    for k in (1, 2, 3):
        table["qz", k] = lambda k=k: same(wq.at[y, x, c, rows(z)], ZP[k])
        table["oz", k] = lambda k=k: same(wo.at[y, x, c, rows(z)], ZP[k])
    for k in range(4):
        table["qx", k] = lambda k=k: same(wq.at[y, x, c, rows(zs[(-k) % 4])], XP)
        table["qy", k] = lambda k=k: same(wq.at[y, x, c, rows(zs[(-k) % 4])], YP)
        if k < 2:
            table["qr", k] = lambda k=k: same(wq.at[y, xx, c, rows(zs[(-k) % 4])], YP)
        else:
            table["qr", k] = lambda k=k: same(wq.at[yy, x, c, rows(zs[(-k) % 4])], XP)
    spots = {"me": lambda: (y, x), "x": lambda: (y, xx), "y": lambda: (yy, x), "d": lambda: (yy, xx)}
    for name, spot in spots.items():
        table["qs", name] = lambda spot=spot: same(wq.at[(*spot(), c)], SB)
        table["os", name] = lambda spot=spot: same(wo.at[(*spot(), c)], SB)
    table["ox"] = lambda: same(wo.at[y, x, c], XP)
    table["oy"] = lambda: same(wo.at[y, x, c], YP)
    table["orx"] = lambda: same(wo.at[y, xx, c, pl.ds(0, 32)], YP)
    table["ory"] = lambda: same(wo.at[yy, x, c, pl.ds(32, 32)], XP)
    for s in range(STEPS):
        for k in (1, 2, 3):
            table["fz", s, k] = lambda s=s, k=k: (
                win.at[:, cols(zs[(k + s) % 4])],
                wf.at[s, y, x, c, rows(z)],
                ZP[k],
            )
        if s:
            table["fo", s] = lambda s=s: (wout, wf.at[s, y, x, c, pl.ds(64, 64)], ZP[4 - s])
        table["fx", s] = lambda s=s: same(wf.at[s, y, x, c], XP)
        table["fy", s] = lambda s=s: same(wf.at[s, y, x, c], YP)
        table["frx", s] = lambda s=s: same(wf.at[s, y, xx, c, pl.ds(0, 64)], YP)
        table["fry", s] = lambda s=s: same(wf.at[s, yy, x, c, pl.ds(64, 64)], XP)
        for name, spot in spots.items():
            table["fs", s, name] = lambda s=s, spot=spot: same(wf.at[(s, *spot(), c)], SB)
    table["tok"] = lambda: (xrow.at[pl.ds(0, 512)], xrow.at[pl.ds(512, 512)], SB)
    groups = {}
    for s in range(STEPS):
        groups["f", s] = (gf.at[s], rcf.at[s], s1f.at[s], r1f.at[s], s2f.at[s], r2f.at[s], s3f.at[s], r3f.at[s])
        if s:
            table["o3", s] = lambda s=s: (s3o.at[s - 1], r3o.at[s - 1], ZP[s])
    groups["o"] = (go, rco, s1o, r1o, s2o, r2o, s3w, r3w)
    for p in range(PAIRS):
        gq = gf.at[p, :, :, :, pl.ds(0, 64), pl.ds(0, 384)]
        rcq = rcf.at[p, :, :, pl.ds(0, 64), pl.ds(0, 384)]
        groups["q", p] = (gq, rcq, s1q.at[p], r1q.at[p], s2q.at[p], r2q.at[p], s3q.at[p], r3q.at[p])
        table["kv", p] = lambda p=p: (dkv.at[p % 2, :, :, pl.ds(512, 512)], rkv.at[p], SB)
    for g, (grad, rc, s1, r1, s2, r2, s3, r3) in groups.items():
        table["c", g] = lambda grad=grad, rc=rc: (grad.at[:, :, cc], rc, SB)
        table["a1", g] = lambda s1=s1, r1=r1: (s1.at[0], r1.at[0], XP)
        table["b1", g] = lambda s1=s1, r1=r1: (s1.at[1], r1.at[1], YP)
        table["a2", g] = lambda s2=s2, r2=r2: (s2.at[0], r2.at[0], YP)
        table["b2", g] = lambda s2=s2, r2=r2: (s2.at[1], r2.at[1], XP)
        for k in (1, 2, 3):
            table["z3", g, k] = lambda s3=s3, r3=r3, k=k: (s3.at[k - 1], r3.at[k - 1], ZP[k])
    table["bc"] = lambda: (bb.at[0], rb.at[0], SB)
    table["bx"] = lambda: (bb.at[1], rb.at[1], XP)
    table["by"] = lambda: (bb.at[2], rb.at[2], YP)
    for k in (1, 2, 3):
        table["bz", k] = lambda k=k: (bb.at[3], rb.at[2 + k], ZP[k])
    for place, key in enumerate(table):
        ids[key] = place

    def cp(*key):
        key = key if len(key) > 1 else key[0]
        src, dst, dev = table[key]()
        place = ids[key]
        return pltpu.make_async_remote_copy(
            src_ref=src,
            dst_ref=dst,
            send_sem=send_sem.at[place],
            recv_sem=recv_sem.at[place],
            device_id=dev,
            device_id_type=MESH,
        )

    def start(*key):
        cp(*key).start()

    def recv(*key):
        cp(*key).wait_recv()

    local = [
        (wcat, wq.at[y, x, c, rows(z)]),
        (tok, xrow.at[pl.ds(0, 512)]),
        (cot, cotv),
        (wout_proj, wo.at[y, x, c, rows(z)]),
        (wout, wf.at[0, y, x, c, pl.ds(64, 64)]),
    ] + [(win.at[:, cols(zs[s])], wf.at[s, y, x, c, rows(z)]) for s in range(STEPS)]
    local = [pltpu.make_async_copy(src, dst, local_sem.at[i]) for i, (src, dst) in enumerate(local)]
    for one in local:
        one.start()
    barrier = pltpu.get_barrier_semaphore()
    for dev in (XP, YP, ZP[1], ZP[2], ZP[3], SB):
        pl.semaphore_signal(barrier, inc=1, device_id=dev, device_id_type=MESH)
    pl.semaphore_wait(barrier, 6)

    local[0].wait()
    for k in (1, 2, 3):
        start("qz", k)
    start("qx", 0)
    start("qy", 0)
    local[1].wait()
    start("tok")

    own_seg = seg[:, pl.ds(pl.multiple_of(c * 512, 512), 512)].astype(F32)
    sib_seg = seg[:, pl.ds(pl.multiple_of(cc * 512, 512), 512)].astype(F32)
    used = fill[0]
    for block in range(8):
        half, inside = block // 4, block % 4
        part = (own_seg if half == 0 else sib_seg)[:, inside * 128 : inside * 128 + 128]
        seg_keys = jnp.broadcast_to(part, (128, 128)).T
        seg_keys = jnp.concatenate([seg_keys] * 4, axis=1)
        base = (c if half == 0 else cc) * 512 + inside * 128
        key_at = lax.broadcasted_iota(jnp.int32, (128, 512), 0) + base
        query_at = lax.broadcasted_iota(jnp.int32, (128, 512), 1) + c * 512
        allowed = (seg_keys == own_seg) & ((key_at < used) | (key_at == query_at))
        maskb[block * 128 : block * 128 + 128, :] = jnp.where(allowed, 0.0, -1e30)

    gate_attn = gates[0]
    gate_feed = gates[1]
    local[2].wait()
    upstream = cotv[...].astype(F32)
    gffn[...] = (gate_feed * upstream).astype(BF)

    for k in (1, 2, 3):
        recv("qz", k)
        start("qx", k)
        start("qy", k)
    start("qs", "me")
    for one in local[3:]:
        one.wait()
    for k in (1, 2, 3):
        start("oz", k)
    for s in range(STEPS):
        for k in (1, 2, 3):
            start("fz", s, k)
        if s:
            start("fo", s)
    for k in (0, 1):
        recv("qx", k)
        start("qr", k)
    for k in (2, 3):
        recv("qy", k)
        start("qr", k)
    recv("qx", 2)
    recv("qx", 3)
    start("qs", "x")
    recv("qy", 0)
    recv("qy", 1)
    start("qs", "y")
    for k in (1, 2, 3):
        recv("oz", k)
    start("ox")
    start("oy")
    start("os", "me")
    for k in range(4):
        recv("qr", k)
    start("qs", "d")

    def plane_first(s):
        for k in (1, 2, 3):
            recv("fz", s, k)
        if s:
            recv("fo", s)
        start("fx", s)
        start("fy", s)
        start("fs", s, "me")

    def plane_second(s):
        recv("fx", s)
        start("frx", s)
        start("fs", s, "x")
        recv("fy", s)
        start("fry", s)
        start("fs", s, "y")

    def plane_third(s):
        recv("frx", s)
        recv("fry", s)
        start("fs", s, "d")

    def all_here(s):
        for name in spots:
            recv("fs", s, name)

    plane_first(0)
    for name in spots:
        recv("qs", name)
    recv("tok")

    held = wq[:, :, :, :, pl.ds(1536, 128)].reshape(8, 4, 16, 128).transpose(1, 0, 2, 3).reshape(32, 16, 128)
    biasb[...] = jnp.sum(held.astype(F32), axis=1).astype(BF)

    def bias_row(offset, per, width):
        lane = lax.broadcasted_iota(jnp.int32, (128, width), 0)
        at = lax.broadcasted_iota(jnp.int32, (128, width), 1)
        pick = (lane == offset + lax.rem(at, per)).astype(F32).astype(BF)
        spread = dot(biasb[...], pick, 1, 0)
        owner = lax.broadcasted_iota(jnp.int32, (32, width), 0)
        at = lax.broadcasted_iota(jnp.int32, (32, width), 1)
        return jnp.sum(jnp.where(owner == lax.div(at, per), spread, 0.0), axis=0, keepdims=True)

    first_row = lax.broadcasted_iota(jnp.int32, (16, 512), 0) == 0
    ones_row = jnp.where(first_row, 1.0, 0.0).astype(BF)

    def as_rank_one(row):
        return jnp.where(first_row, jnp.broadcast_to(row, (16, 512)), 0.0).astype(BF)

    bias_q = as_rank_one(bias_row(0, 16, 512))
    bias_v = as_rank_one(bias_row(16, 16, 512))
    for p in range(PAIRS):
        at = slice(p * 128, p * 128 + 128)
        weights = natural(wq[:, :, :, :, p * 384 : p * 384 + 384])
        ours = dot(weights, xrow[0:512], 0, 1)
        theirs = dot(weights[:, 128:384], xrow[512:1024], 0, 1)
        add_q = dot(bias_q[:, at], ones_row, 0, 0)
        add_v = dot(bias_v[:, at], ones_row, 0, 0)
        qt[at] = ((ours[0:128] + add_q).astype(BF).astype(F32) * 0.125).astype(BF)
        kt[at, 0:512] = ours[128:256].astype(BF)
        vt[at, 0:512] = (ours[256:384] + add_v).astype(BF)
        kt[at, 512:1024] = theirs[0:128].astype(BF)
        vt[at, 512:1024] = (theirs[128:256] + add_v).astype(BF)

    def o_second():
        recv("ox")
        start("orx")
        start("os", "x")
        recv("oy")
        start("ory")
        start("os", "y")

    def o_third():
        recv("orx")
        recv("ory")
        start("os", "d")

    o_second()
    plane_first(1)

    def forward_pair(p, carry):
        for j in range(2):
            head = p * 2 + j
            at = pl.ds(pl.multiple_of(head * 64, 64), 64)
            keys, values = kt[at], vt[at]
            for part in range(2):
                lanes = slice(part * 256, part * 256 + 256)
                raw = dot(keys, qt[at, lanes], 0, 0)
                highest = jnp.full((8, 256), -jnp.inf, F32)
                for b in range(8):
                    r = slice(b * 128, b * 128 + 128)
                    score = raw[r] + maskb[r, lanes]
                    st[r, lanes] = score
                    highest = jnp.maximum(highest, jnp.max(score.reshape(16, 8, 256), axis=0))
                highest = jnp.max(highest, axis=0, keepdims=True)
                total = jnp.zeros((8, 256), F32)
                for b in range(8):
                    r = slice(b * 128, b * 128 + 128)
                    expo = jnp.exp(st[r, lanes] - highest)
                    st[r, lanes] = expo
                    total = total + jnp.sum(expo.reshape(16, 8, 256), axis=0)
                scale = 1.0 / jnp.sum(total, axis=0, keepdims=True)
                for b in range(8):
                    r = slice(b * 128, b * 128 + 128)
                    prob = st[r, lanes] * scale
                    probs[head, r, lanes] = prob
                    pb[0, r, lanes] = prob.astype(BF)
                mixt[at, lanes] = dot(values, pb[0, :, lanes], 1, 0).astype(BF)

        @pl.when(p == 0)
        def _():
            o_third()

        @pl.when(p == 1)
        def _():
            plane_second(0)

        @pl.when(p == 2)
        def _():
            plane_first(2)

        @pl.when(p == 3)
        def _():
            plane_second(1)
            plane_first(3)

        return carry

    lax.fori_loop(0, PAIRS, forward_pair, 0)

    for name in spots:
        recv("os", name)
    attn[...] = dot(mixt[...], natural(wo[...]), 0, 0) + bias_row(32, 16, 512)
    resid = xrow[0:512].astype(F32) + gate_attn * attn[...]
    rlow[...] = resid.astype(BF)
    ffn[...] = jnp.zeros((512, 512), F32)
    gres[...] = cotv[...].astype(F32)

    def fold_first(g):
        grad, rc, s1 = groups[g][:3]
        half = rc.shape[2] // 2
        recv("c", g)
        for i in range(2):
            s1[0, i] = (grad[i, xx, c, 0:half] + rc[i, xx, 0:half]).astype(BF)
            s1[1, i] = (grad[yy, i, c, half : 2 * half] + rc[yy, i, half : 2 * half]).astype(BF)
        start("a1", g)
        start("b1", g)

    def fold_second(g):
        grad, rc, s1, r1, s2, r2 = groups[g][:6]
        half = rc.shape[2] // 2
        recv("a1", g)
        s2[0] = (grad[yy, x, c, 0:half] + rc[yy, x, 0:half] + r1[0, yy].astype(F32)).astype(BF)
        start("a2", g)
        recv("b1", g)
        s2[1] = (
            grad[y, xx, c, half : 2 * half] + rc[y, xx, half : 2 * half] + r1[1, xx].astype(F32)
        ).astype(BF)
        start("b2", g)

    def fold_third(g):
        grad, rc, s1, r1, s2, r2, s3, r3 = groups[g]
        half = rc.shape[2] // 2
        width = rc.shape[3]
        recv("a2", g)
        upper = grad[y, x, c, 0:half] + rc[y, x, 0:half] + r1[0, y].astype(F32) + r2[0].astype(F32)
        ksum[0:half, 0:width] = upper
        recv("b2", g)
        lower = (
            grad[y, x, c, half : 2 * half]
            + rc[y, x, half : 2 * half]
            + r1[1, x].astype(F32)
            + r2[1].astype(F32)
        )
        ksum[half : 2 * half, 0:width] = lower
        for k in (1, 2, 3):
            s3[k - 1] = ksum[rows(zs[k]), 0:width].astype(BF)
            start("z3", g, k)

    def ffn_third(s):
        fold_third(("f", s))
        gi_o[:, cols(zs[s])] = ksum[rows(z), :]
        if s:
            s3o[s - 1] = ksum[64:128].astype(BF)
            start("o3", s)
        else:
            gout_o[...] = ksum[64:128]

    def small(row, value):
        bb[0, row : row + 1, 0:512] = value

    bb[0, :, 512:640] = jnp.zeros((8, 128), F32)

    def ffn_step(s):
        plane_third(s)
        all_here(s)
        inner = natural(wf[s, :, :, :, 0:64])
        outer = wf[s, :, :, :, 64:128].reshape(512, 512)
        hid[...] = dot(rlow[...], inner, 1, 0) + chunk_bias[s]
        gac[...] = dot(gffn[...], outer, 1, 1)
        for b in range(8):
            r = slice(b * 64, b * 64 + 64)
            value, slope = gelu_parts(hid[r])
            act[r] = value.astype(BF)
            ghid[r] = (gac[r] * slope).astype(BF)
        ffn[...] += dot(act[...], outer, 1, 0)
        gf[s, :, :, :, 64:128] = dot(act[...], gffn[...], 0, 0).reshape(2, 2, 2, 64, 512)
        gf[s, :, :, :, 0:64] = by_chip(dot(rlow[...], ghid[...], 0, 0))
        start("c", ("f", s))
        gres[...] += dot(ghid[...], inner, 1, 1)
        sums = col_sums(ghid[...])[0:1]
        for row in range(4):
            bb[0, 4 + row : 5 + row, 0:512] = jnp.where(
                zs[s] == row, sums, bb[0, 4 + row : 5 + row, 0:512]
            )

    inner_bias = bias_row(64, 64, 2048)
    parts = [inner_bias[:, i * 512 : i * 512 + 512] for i in range(4)]
    chunk_bias = []
    for s in range(STEPS):
        picked = parts[3]
        for i in range(3):
            picked = jnp.where(zs[s] == i, parts[i], picked)
        chunk_bias.append(picked)
    for row in range(4):
        small(4 + row, jnp.zeros((1, 512), F32))

    ffn_step(0)
    plane_second(2)
    ffn_step(1)
    fold_first(("f", 0))
    plane_second(3)
    ffn_step(2)
    fold_first(("f", 1))
    fold_second(("f", 0))
    ffn_step(3)
    fold_first(("f", 2))
    fold_second(("f", 1))
    ffn_third(0)

    ffn[...] += bias_row(48, 16, 512)
    upstream = cotv[...].astype(F32)
    resid = xrow[0:512].astype(F32) + gate_attn * attn[...]
    rlow[...] = (resid + gate_feed * ffn[...]).astype(BF)
    layer_out = pltpu.make_async_copy(rlow, layer_o, local_sem.at[0])
    layer_out.start()
    feed_part = jnp.sum(jnp.sum(upstream * ffn[...], axis=0, keepdims=True), axis=1, keepdims=True)
    attn_part = jnp.sum(jnp.sum(gres[...] * attn[...], axis=0, keepdims=True), axis=1, keepdims=True)
    bb[0, 0:1, 512:640] = jnp.broadcast_to(attn_part, (1, 128))
    bb[0, 1:2, 512:640] = jnp.broadcast_to(feed_part, (1, 128))
    small(3, col_sums(gffn[...])[0:1])
    gattn = (gate_attn * gres[...]).astype(BF)
    small(2, col_sums(gattn)[0:1])
    go[...] = by_chip(dot(mixt[...], gattn, 1, 0))
    start("c", "o")
    gmixt[...] = dot(natural(wo[...]), gattn, 1, 1).astype(BF)

    def backward_pair(p, carry):
        slot = lax.rem(p, 2)
        for j in range(2):
            head = p * 2 + j
            at = pl.ds(pl.multiple_of(head * 64, 64), 64)
            keys, values = kt[at], vt[at]
            for part in range(2):
                lanes = slice(part * 256, part * 256 + 256)
                up = gmixt[at, lanes]
                raw = dot(values, up, 0, 0)
                total = jnp.zeros((8, 256), F32)
                for b in range(8):
                    r = slice(b * 128, b * 128 + 128)
                    block = raw[r]
                    st[r, lanes] = block
                    total = total + jnp.sum((probs[head, r, lanes] * block).reshape(16, 8, 256), axis=0)
                inner = jnp.sum(total, axis=0, keepdims=True)
                for b in range(8):
                    r = slice(b * 128, b * 128 + 128)
                    prob = probs[head, r, lanes]
                    pb[0, r, lanes] = prob.astype(BF)
                    pb[1, r, lanes] = (prob * (st[r, lanes] - inner)).astype(BF)
                dqt[slot, j * 64 : j * 64 + 64, lanes] = (
                    dot(keys, pb[1, :, lanes], 1, 0) * 0.125
                ).astype(BF)
                grad_k = dot(qt[at, lanes], pb[1, :, lanes], 1, 1)
                grad_v = dot(up, pb[0, :, lanes], 1, 1)
                place = slice(j * 64, j * 64 + 64)
                if part == 0:
                    dkv[slot, 0, place] = grad_k
                    dkv[slot, 1, place] = grad_v
                else:
                    dkv[slot, 0, place] += grad_k
                    dkv[slot, 1, place] += grad_v
        return carry

    def finish_pair(p):
        slot = p % 2
        recv("kv", p)
        grad_k = (dkv[slot, 0, :, 0:512] + rkv[p, 0]).astype(BF)
        grad_v = (dkv[slot, 1, :, 0:512] + rkv[p, 1]).astype(BF)
        both = jnp.concatenate([dqt[slot], grad_k, grad_v], axis=0)
        cp("c", ("f", p)).wait_send()
        gf[p, :, :, :, 0:64, 0:384] = by_chip(dot(xrow[0:512], both, 0, 1))
        start("c", ("q", p))
        weights = natural(wq[:, :, :, :, p * 384 : p * 384 + 384])
        gres[...] += dot(both, weights, 0, 1)
        sums = dot(jnp.ones((8, 512), BF), both, 1, 1)
        bb[0, 0:1, p * 128 : p * 128 + 128] = sums[0:1, 0:128]
        bb[0, 1:2, p * 128 : p * 128 + 128] = sums[0:1, 256:384]

    for p in range(PAIRS):
        if p >= 2:
            cp("kv", p - 2).wait_send()
        lax.fori_loop(p, p + 1, backward_pair, 0)
        start("kv", p)
        if p == 0:
            fold_first(("f", 3))
            fold_second(("f", 2))
            ffn_third(1)
            fold_first("o")
        if p == 1:
            finish_pair(0)
            fold_second(("f", 3))
            ffn_third(2)
            fold_second("o")
        if p == 2:
            finish_pair(1)
            fold_first(("q", 0))
            ffn_third(3)
            fold_third("o")
            go_o[...] = ksum[rows(z), :]
        if p == 3:
            finish_pair(2)
            fold_first(("q", 1))
            fold_second(("q", 0))
    finish_pair(3)
    tg_out = pltpu.make_async_copy(gres, tg_o, local_sem.at[1])
    tg_out.start()

    start("bc")

    def q_third(p):
        fold_third(("q", p))
        at = slice(p * 128, p * 128 + 128)
        gq_o[:, at] = ksum[rows(z), 0:128]
        gk_o[:, at] = ksum[rows(z), 128:256]
        gv_o[:, at] = ksum[rows(z), 256:384]

    def q_last(p):
        at = slice(p * 128, p * 128 + 128)
        for k in (1, 2, 3):
            recv("z3", ("q", p), k)
        more = r3q[p, 0].astype(F32) + r3q[p, 1].astype(F32) + r3q[p, 2].astype(F32)
        gq_o[:, at] += more[:, 0:128]
        gk_o[:, at] += more[:, 128:256]
        gv_o[:, at] += more[:, 256:384]

    recv("bc")
    bb[1] = bb[0] + rb[0]
    start("bx")
    fold_first(("q", 2))
    fold_first(("q", 3))
    fold_second(("q", 1))
    q_third(0)
    recv("bx")
    bb[2] = bb[1] + rb[1]
    start("by")
    fold_second(("q", 2))
    fold_second(("q", 3))
    q_third(1)
    recv("by")
    bb[3] = bb[2] + rb[2]
    for k in (1, 2, 3):
        start("bz", k)
    q_third(2)
    q_third(3)

    for s in range(STEPS):
        for k in (1, 2, 3):
            recv("z3", ("f", s), k)
    for s in range(STEPS):
        more = r3f[(s + 1) % 4, 0].astype(F32)
        for k in (2, 3):
            more = more + r3f[(s + k) % 4, k - 1].astype(F32)
        gi_o[:, cols(zs[s])] += more
    for s in (1, 2, 3):
        recv("o3", s)
        gout_o[...] += r3o[s - 1].astype(F32)
    for k in (1, 2, 3):
        recv("z3", "o", k)
        go_o[...] += r3w[k - 1].astype(F32)
    for p in range(PAIRS):
        q_last(p)
    for k in (1, 2, 3):
        recv("bz", k)
    total = bb[3] + rb[3] + rb[4] + rb[5]
    device = lo * 2 + c
    narrow = pltpu.roll(total[:, 0:512], lax.rem(512 - device * 16, 512), 1)
    wide = pltpu.roll(total[:, 0:512], lax.rem(512 - lax.rem(device, 8) * 64, 512), 1)
    owner = lax.broadcasted_iota(jnp.int32, (8, 128), 0) == 4 + lax.div(device, 8)
    small_o[0:4] = narrow[0:4, 0:128]
    small_o[4:5] = jnp.sum(jnp.where(owner, wide[:, 0:128], 0.0), axis=0, keepdims=True)
    small_o[5:7] = total[0:2, 512:640]
    small_o[7:8] = jnp.zeros((1, 128), F32)

    layer_out.wait()
    tg_out.wait()
    waited = {("kv", 0), ("kv", 1)} | {("c", ("f", p)) for p in range(PAIRS)}
    for key in table:
        if key not in waited:
            (cp(*key) if isinstance(key, tuple) else cp(key)).wait_send()


def scratch():
    v = pltpu.VMEM
    return [
        v((1024, 512), BF),
        v((512, 512), BF),
        v((2, 2, 2, 64, 1664), BF),
        v((2, 2, 2, 64, 512), BF),
        v((4, 2, 2, 2, 128, 512), BF),
        v((1024, 512), F32),
        v((512, 512), BF),
        v((512, 1024), BF),
        v((512, 1024), BF),
        v((8, 1024, 512), F32),
        v((1024, 512), F32),
        v((2, 1024, 512), BF),
        v((512, 512), BF),
        v((512, 512), F32),
        v((512, 512), BF),
        v((512, 512), BF),
        v((512, 512), BF),
        v((2, 128, 512), BF),
        v((2, 2, 128, 1024), F32),
        v((4, 2, 128, 512), F32),
        v((4, 2, 2, 2, 128, 512), F32),
        v((4, 2, 2, 128, 512), F32),
        v((4, 2, 2, 64, 512), BF),
        v((4, 2, 2, 64, 512), BF),
        v((4, 2, 64, 512), BF),
        v((4, 2, 64, 512), BF),
        v((4, 3, 16, 512), BF),
        v((4, 3, 16, 512), BF),
        v((3, 64, 512), BF),
        v((3, 64, 512), BF),
        v((2, 2, 2, 64, 512), F32),
        v((2, 2, 64, 512), F32),
        v((2, 2, 32, 512), BF),
        v((2, 2, 32, 512), BF),
        v((2, 32, 512), BF),
        v((2, 32, 512), BF),
        v((3, 16, 512), BF),
        v((3, 16, 512), BF),
        v((4, 2, 2, 32, 384), BF),
        v((4, 2, 2, 32, 384), BF),
        v((4, 2, 32, 384), BF),
        v((4, 2, 32, 384), BF),
        v((4, 3, 16, 384), BF),
        v((4, 3, 16, 384), BF),
        v((128, 512), F32),
        v((4, 8, 640), F32),
        v((6, 8, 640), F32),
        v((32, 128), BF),
        pltpu.SemaphoreType.DMA((192,)),
        pltpu.SemaphoreType.DMA((192,)),
        pltpu.SemaphoreType.DMA((9,)),
    ]


def on_device(
    tokens,
    segments,
    fill_length,
    query_weight,
    key_weight,
    value_weight,
    output_weight,
    query_bias,
    value_bias,
    output_bias,
    inner_weight,
    inner_bias,
    outer_weight,
    outer_bias,
    residual_gates,
    cotangent,
):
    names = ("dp", "shard")
    several = lax.axis_size("dp") > GROUP
    place = lax.rem(lax.axis_index("dp"), GROUP) * 2 + lax.axis_index("shard")

    def block_of(shard):
        if not several:
            return shard
        whole = lax.all_gather(shard, names, axis=0, tiled=True)
        rows = whole.shape[0] // (2 * GROUP)
        return lax.dynamic_slice_in_dim(whole, place * rows, rows, 0)

    def owned(block):
        if not several:
            return block
        rows = block.shape[0]
        whole = jnp.zeros((rows * 2 * GROUP, *block.shape[1:]), F32)
        whole = lax.dynamic_update_slice_in_dim(whole, block, place * rows, 0)
        return lax.psum_scatter(whole, names, scatter_dimension=0, tiled=True)

    query_weight, key_weight, value_weight, output_weight, inner_weight, outer_weight = map(
        block_of, (query_weight, key_weight, value_weight, output_weight, inner_weight, outer_weight)
    )
    query_bias, value_bias, output_bias, inner_bias, outer_bias = map(
        block_of, (query_bias, value_bias, output_bias, inner_bias, outer_bias)
    )
    pieces = []
    for p in range(PAIRS):
        for weight in (query_weight, key_weight, value_weight):
            pieces.append(weight[:, p * 128 : p * 128 + 128])
    bias = jnp.concatenate([query_bias, value_bias, output_bias, outer_bias, inner_bias])[None, :]
    pieces.append(jnp.pad(bias, ((0, 15), (0, 0))))
    wcat = jnp.concatenate(pieces, axis=1)
    vmem = pl.BlockSpec(memory_space=pltpu.VMEM)
    smem = pl.BlockSpec(memory_space=pltpu.SMEM)
    hbm = pl.BlockSpec(memory_space=pl.ANY)
    shape = jax.ShapeDtypeStruct
    outs = pl.pallas_call(
        layer_kernel,
        out_shape=[
            shape((512, 512), BF),
            shape((512, 512), F32),
            shape((16, 512), F32),
            shape((16, 512), F32),
            shape((16, 512), F32),
            shape((16, 512), F32),
            shape((16, 2048), F32),
            shape((64, 512), F32),
            shape((8, 128), F32),
        ],
        in_specs=[hbm, hbm, vmem, smem, smem, hbm, hbm, hbm, hbm],
        out_specs=[hbm, hbm] + [vmem] * 7,
        scratch_shapes=scratch(),
        compiler_params=pltpu.CompilerParams(
            collective_id=0, has_side_effects=True, vmem_limit_bytes=64 * 2**20 - 2**17
        ),
    )(
        tokens.reshape(512, 512),
        cotangent.reshape(512, 512),
        segments,
        fill_length,
        residual_gates,
        wcat,
        output_weight,
        inner_weight,
        outer_weight,
    )
    layer, token_grads, gq, gk, gv, go, gi, gout, small = outs
    gate_sums = small[5:7, 0]
    if several:
        gate_sums = lax.psum(jnp.where(place == 0, gate_sums, 0.0), names)
    grads = (
        gq,
        gk,
        gv,
        go,
        small[0, 0:16],
        small[1, 0:16],
        small[2, 0:16],
        gi,
        small[4, 0:64],
        gout,
        small[3, 0:16],
    )
    return (layer[None], token_grads[None], *map(owned, grads), gate_sums)


def solution(mesh):
    spread = P(("dp", "shard"))
    return jax.shard_map(
        on_device,
        mesh=mesh,
        in_specs=(
            P("dp", "shard", None),
            P("dp", None),
            P("dp"),
            *([P(("dp", "shard"), None)] * 4),
            *([spread] * 3),
            P(("dp", "shard"), None),
            spread,
            P(("dp", "shard"), None),
            spread,
            P(),
            P("dp", "shard", None),
        ),
        out_specs=(
            P("dp", "shard", None),
            P("dp", "shard", None),
            *([P(("dp", "shard"), None)] * 4),
            *([spread] * 3),
            P(("dp", "shard"), None),
            spread,
            P(("dp", "shard"), None),
            spread,
            P(),
        ),
        check_vma=False,
    )
```

time: 1190 us -> 119 us (0.10); the launches traced: 1180 us -> 118 us
  waiting for transfers between devices: 721 us -> 0 us
  blocking collectives: 257 us -> 0 us
  Pallas kernels: 0 us -> 102 us
  matrix products: 92.4 us -> 0 us
  local copies, waits for them, and re-layouts: 65.8 us -> 14.7 us
  starting transfers between devices: 15.3 us -> 0 us
  between operations: 15.8 us -> 1.41 us
    reduce_scatter x3 -> x0, waiting for transfers between devices: 413 us -> none  [the longest x1 140 us: on_device(): lax.psum_scatter(grad_inner_w, ('dp', 'shard'), scatter_dimension=0, tile...]
    unnamed x11 -> x0, waiting for transfers between devices: 305 us -> none
    all_gather x4 -> x0, blocking collectives: 159 us -> none  [the longest x1 42.1 us: on_device(): lax.all_gather(query_weight, ('dp', 'shard'), axis=0, tiled=True)]
    pallas_call x0 -> x1, Pallas kernels: none -> 102 us  [on_device(): pl.pallas_call(layer_kernel, out_shape=[shape((512, 512), BF), shape((512...]
    dot_general x46 -> x0, matrix products: 92.4 us -> none  [the longest x1 13.7 us: on_device(): jnp.dot(resid_low, inner_full, preferred_element_type=jnp.float32)]
    unnamed x2 -> x0, blocking collectives: 79.6 us -> none
    unnamed x77 -> x52, local copies, waits for them, and re-layouts: 34.9 us -> 10.7 us
    all_to_all x4 -> x0, blocking collectives: 18.3 us -> none  [the longest x1 5.11 us: on_device(): lax.all_to_all(grad_attended, 'shard', split_axis=2, concat_axis=1, tiled...]
  transfers between devices with their start and end apart: 12 -> 0, of which waited for: 8 -> 0; matrix products, arithmetic and copies ran while one was open for 9% -> 0% of each run, Pallas kernels for 0% -> 0%
where the time goes in v1:
time: 119 us; the launch traced here: 118 us
  Pallas kernels  102 us (86%)
  local copies, waits for them, and re-layouts  14.7 us (12%)
  between operations  1.41 us (1%)
    pallas_call x1, Pallas kernels, on_device(): pl.pallas_call(layer_kernel, out_shape=[shape((512, 512), BF), shape((512...  102 us
    unnamed x52, local copies, waits for them, and re-layouts  10.7 us

profile of v1, /device:TPU:0, one launch (start us, length us, event | category | flops | bytes accessed | tf_op | source)
XLA Modules:
  0.0 118.2 jit_solution(9694027203413863779)
XLA Ops:
  0.6 0.0 copy-start.8
  0.7 0.8 constant_dynamic-update-slice_fusion.12
  1.4 0.0 copy-start.10
  1.4 0.7 constant_dynamic-update-slice_fusion.11
  2.1 0.7 constant_dynamic-update-slice_fusion.10
  2.8 0.0 copy-done.8
  2.8 0.0 copy-start.9
  2.8 0.8 constant_dynamic-update-slice_fusion.8
  3.6 0.0 copy-done.10
  3.6 0.0 copy-done.9
  3.7 0.0 copy-start.11
  3.7 0.0 copy-start.12
  3.7 0.0 copy-start.13
  3.7 0.0 copy-start.14
  3.7 0.0 copy-start.15
  3.7 0.6 copy-done.11
  4.3 0.0 copy-done.12
  4.3 0.0 copy-done.13
  4.3 0.0 copy-done.14
  4.4 0.0 copy-done.15
  4.4 0.1 concatenate.6
  4.5 0.0 copy-start.3
  5.1 0.0 copy-done.3
  5.1 102.1 %shard_map.263 = (bf16[512,512]{1,0:T(8,128)(2,1)}, f32[512,512]{1,0:T(8,128)}, f32[16,512]{1,0:T(8,128)}, f32[16,512]{1,0:T(8,128)}, f32[16,512]{1,0:T(8,128)},...) custom-call(bf16[512,512]{1,0:T(8,128)(2,1)} %bitcast.16, ...), custom_call_target="tpu_custom_call" | custom-call | tf_op jit(solution)/shard_map/pallas_call | solution.py:834
  107.2 0.0 copy-start
  107.2 1.4 %slice_bitcast_fusion = (f32[16]{0:T(128)}, f32[16]{0:T(128)}, f32[16]{0:T(128)}, f32[16]{0:T(128)}) fusion(f32[8,128]{1,0:T(8,128)} %get-tuple-element.29), kind=kLoop, calls=%fused_computation.14 | loop fusion | bytes 512 | tf_op jit(solution)/shard_map/squeeze | solution.py:879
  108.6 1.2 %slice_bitcast_fusion.1 = f32[64]{0:T(128)} fusion(f32[8,128]{1,0:T(8,128)} %get-tuple-element.29), kind=kLoop, calls=%fused_computation.15 | loop fusion | bytes 512 | tf_op jit(solution)/shard_map/squeeze | solution.py:877
  109.8 1.3 %slice_reduce_fusion = f32[2]{0:T(128)} fusion(f32[8,128]{1,0:T(8,128)} %get-tuple-element.29), kind=kLoop, calls=%fused_computation.13 | loop fusion | bytes 16 | tf_op jit(solution)/shard_map/slice | solution.py:865
  111.1 1.9 %copy.51 = bf16[1,512,512]{2,1,0:T(8,128)(2,1)} copy(bf16[1,512,512]{2,1,0:T(8,128)(2,1)} %bitcast.18) | data formatting | bytes 1048576
  113.0 0.0 copy-done
  113.0 0.0 copy-start.7
  113.0 0.0 copy-start.6
  113.0 0.0 copy-start.5
  113.0 1.0 copy.52
  114.0 0.0 copy-done.7
  114.0 0.0 copy-start.2
  114.0 0.6 copy.53
  114.6 0.0 copy-done.6
  114.6 0.6 copy.54
  115.2 0.0 copy-done.5
  115.2 0.0 copy-start.4
  115.2 0.6 copy.55
  115.8 0.2 copy-done.4
  116.0 0.6 copy.56
  116.6 0.0 copy-done.2
  116.6 0.7 copy.57
  117.2 0.3 copy-done.1
  117.5 0.7 copy.58
  (10 shorter events, 0.1 us)
Async XLA Ops:
  0.6 2.2 %copy-start.8 = (bf16[16,512]{1,0:T(8,128)(2,1)S(1)}, bf16[16,512]{1,0:T(8,128)(2,1)}, u32[]{:S(2)}) copy-start(bf16[16,512]{1,0:T(8,128)(2,1)} %param.19) | copy-start | bytes 49156
  1.4 2.2 %copy-start.10 = (bf16[16,512]{1,0:T(8,128)(2,1)S(1)}, bf16[16,512]{1,0:T(8,128)(2,1)}, u32[]{:S(2)}) copy-start(bf16[16,512]{1,0:T(8,128)(2,1)} %param.21) | copy-start | bytes 49156
  2.8 0.8 copy-start.9
  3.7 0.7 copy-start.11
  3.7 0.7 copy-start.12
  3.7 0.7 copy-start.13
  3.7 0.7 copy-start.14
  3.7 0.7 copy-start.15
  4.5 0.7 copy-start.3
  107.2 5.7 %copy-start = (f32[512,512]{1,0:T(8,128)S(1)}, f32[512,512]{1,0:T(8,128)}, u32[]{:S(2)}) copy-start(f32[512,512]{1,0:T(8,128)} %get-tuple-element.24) | copy-start | bytes 3145732
  113.0 1.0 copy-start.7
  113.0 1.6 %copy-start.6 = (f32[16,512]{1,0:T(8,128)S(1)}, f32[16,512]{1,0:T(8,128)}, u32[]{:S(2)}) copy-start(f32[16,512]{1,0:T(8,128)} %get-tuple-element.53) | copy-start | bytes 98308
  113.0 2.2 %copy-start.5 = (f32[16,512]{1,0:T(8,128)S(1)}, f32[16,512]{1,0:T(8,128)}, u32[]{:S(2)}) copy-start(f32[16,512]{1,0:T(8,128)} %get-tuple-element.54) | copy-start | bytes 98308
  114.0 2.6 %copy-start.2 = (f32[16,2048]{1,0:T(8,128)S(1)}, f32[16,2048]{1,0:T(8,128)}, u32[]{:S(2)}) copy-start(f32[16,2048]{1,0:T(8,128)} %get-tuple-element.59) | copy-start | bytes 393220
  115.2 0.8 copy-start.4
  116.6 1.0 copy-start.1

commit v2 on v1

v2 whole, which is shorter than its diff:
```python
import jax
import jax.numpy as jnp
from jax import lax
from jax.experimental import pallas as pl
from jax.experimental.pallas import tpu as pltpu
from jax.sharding import PartitionSpec as P

MESH = pl.DeviceIdType.MESH
BF = jnp.bfloat16
F32 = jnp.float32
HEADS = 8
GROUP = 16
PAIRS = 4
VMEM_BYTES = 64 * 2**20 - 2**17
PLAN = {
    "start": ("1q0", "zq2", "1q1", "zq3", "1q2", "zf0", "2q0", "3q0", "1q3", "zf1", "2q1",),
    "fwd0": ("2q2", "1f0", "zf2",),
    "fwd1": ("2q3",),
    "proj1": ("3q1", "3q2", "1f1", "zf3", "2f0",),
    "fwd2": ("3q3",),
    "proj2": ("1f2",),
    "fwd5": ("2f1",),
    "proj3": ("3f0", "1f3",),
    "outproj": ("2f2",),
    "ffn0": ("3f1",),
    "ffn1": ("2f3",),
    "ffn2": ("3f2", "3f3", "FF0",),
    "ffn3": ("FF1",),
    "pre": ("SF0",),
    "bwd0": ("FF2",),
    "bwd1": ("SF1",),
    "bwd2": ("TF0", "FF3",),
    "bwd3": ("FO", "SF2",),
    "fin0": ("TF1",),
    "bwd5": ("SF3", "FQ0",),
    "fin1": ("SO", "TF2",),
    "bwd6": ("TF3",),
    "bwd7": ("TO", "SQ0", "FQ1",),
    "prod7": ("TQ0", "SQ1",),
    "fin3": ("TQ1", "FQ2",),
    "last1": ("TQ2",),
}
STEPS = 4


def dot(left, right, left_dim, right_dim):
    return lax.dot_general(
        left, right, (((left_dim,), (right_dim,)), ((), ())), preferred_element_type=F32
    )


def gelu_parts(hidden):
    size = jnp.abs(hidden) * 0.7071067811865476
    recip = 1.0 / (1.0 + 0.3275911 * size)
    expo = jnp.exp(-size * size)
    poly = recip * (
        0.127414796
        + recip * (-0.142248368 + recip * (0.7107068705 + recip * (-0.7265760135 + recip * 0.5307027145)))
    )
    tail = poly * expo
    cdf = jnp.where(hidden >= 0, 1.0 - tail, tail)
    return hidden * cdf, cdf + hidden * expo * 0.3989422804014327


def by_chip(value):
    width = value.shape[-1]
    return value.reshape(4, 8, 16, width).transpose(1, 0, 2, 3).reshape(2, 2, 2, 64, width)


def col_sums(value):
    return dot(jnp.ones((8, value.shape[0]), BF), value, 1, 0)


def layer_kernel(
    tok,
    cot,
    seg,
    fill,
    gates,
    bias_q,
    bias_v,
    bias_o,
    bias_out,
    bias_in,
    wquery,
    wkey,
    wvalue,
    wout_proj,
    win,
    wout,
    layer_o,
    tg_o,
    gq_o,
    gk_o,
    gv_o,
    go_o,
    gi_o,
    gout_o,
    small_o,
    xrow,
    cotv,
    wq_rest,
    wq_last,
    wf,
    qt,
    kt,
    vt,
    probs,
    scales,
    st,
    pb,
    mixt,
    attn,
    rlow,
    ffn,
    gres,
    gffn,
    gmixt,
    dqt,
    dkv,
    rkv,
    gf,
    rcf,
    s1f,
    r1f,
    s2f,
    r2f,
    s3f,
    r3f,
    s3o,
    r3o,
    go,
    rco,
    s1o,
    r1o,
    s2o,
    r2o,
    s3w,
    r3w,
    s1q,
    r1q,
    s2q,
    r2q,
    s3q,
    r3q,
    glast,
    rclast,
    s1d,
    r1d,
    ksum,
    bb,
    rb,
    biasb,
    send_sem,
    recv_sem,
    local_sem,
):
    hid, gac = st.at[pl.ds(0, 512)], st.at[pl.ds(512, 512)]
    act, ghid = pb.at[pl.ds(0, 512)], pb.at[pl.ds(512, 512)]
    wq = [wq_rest.at[p] for p in range(PAIRS - 1)] + [wq_last]

    dp = lax.axis_index("dp")
    c = lax.axis_index("shard")
    lo = lax.rem(dp, GROUP)
    z = lax.div(lo, 4)
    y = lax.rem(lax.div(lo, 2), 2)
    x = lax.rem(lo, 2)
    cc, xx, yy = 1 - c, 1 - x, 1 - y

    def zk(k):
        return lax.rem(z + (k % 4), 4)

    zs = [zk(k) for k in range(4)]
    XP = (dp + 1 - 2 * x, c)
    YP = (dp + 2 - 4 * y, c)
    ZP = [None] + [(dp + 4 * (zs[k] - z), c) for k in (1, 2, 3)]
    DP = (dp + 3 - 2 * x - 4 * y, c)
    SB = (dp, cc)

    def rows(place):
        return pl.ds(pl.multiple_of(place * 16, 16), 16)

    def cols(place):
        return pl.ds(pl.multiple_of(place * 512, 512), 512)

    table = {}
    ids = {}

    def same(ref, dev):
        return (ref, ref, dev)

    for p in range(PAIRS):
        for k in (1, 2, 3):
            table["z", ("q", p), k] = lambda p=p, k=k: (
                wq[p].at[y, x, c, pl.ds(0, 16)],
                wq[p].at[y, x, c, pl.ds(k * 16, 16)],
                ZP[k],
            )
        for name, dev in (("x", XP), ("y", YP), ("d", DP)):
            if p == 0 or name != "d":
                for part, (low, count) in enumerate(((0, 16), (16, 48))):
                    table[name, ("q", p), part] = lambda p=p, low=low, count=count, dev=dev: same(
                        wq[p].at[y, x, c, pl.ds(low, count)], dev
                    )
        table["s", ("q", p), 0] = lambda p=p: same(wq[p].at[y, :, c], SB)
        table["s", ("q", p), 1] = lambda p=p: same(wq[p].at[yy, :, c], SB)
        if p:
            table["rx", ("q", p)] = lambda p=p: same(wq[p].at[y, xx, c, pl.ds(0, 32)], YP)
            table["ry", ("q", p)] = lambda p=p: same(wq[p].at[yy, x, c, pl.ds(32, 32)], XP)
    for s in range(STEPS):
        for k in (1, 2, 3):
            table["z", ("f", s), k] = lambda s=s, k=k: (
                win.at[:, cols(zs[(k + s) % 4])],
                wf.at[s, y, x, c, pl.ds(64 + k * 16, 16)],
                ZP[k],
            )
        if s:
            table["zo", ("f", s)] = lambda s=s: (wout, wf.at[s, y, x, c, pl.ds(16, 64)], ZP[4 - s])
        split = 16 if s else 80
        for name, dev in (("x", XP), ("y", YP)):
            for part, (low, count) in enumerate(((0, split), (split, 128 - split))):
                table[name, ("f", s), part] = lambda s=s, low=low, count=count, dev=dev: same(
                    wf.at[s, y, x, c, pl.ds(low, count)], dev
                )
        table["rx", ("f", s)] = lambda s=s: same(wf.at[s, y, xx, c, pl.ds(0, 64)], YP)
        table["ry", ("f", s)] = lambda s=s: same(wf.at[s, yy, x, c, pl.ds(64, 64)], XP)
        table["s", ("f", s), 0] = lambda s=s: same(wf.at[s, y, :, c], SB)
        table["s", ("f", s), 1] = lambda s=s: same(wf.at[s, yy, :, c], SB)
    table["tok"] = lambda: (xrow.at[pl.ds(0, 512)], xrow.at[pl.ds(512, 512)], SB)
    groups = {}
    LAST = (("q", PAIRS - 2), ("q", PAIRS - 1))
    for s in range(STEPS):
        groups["f", s] = (gf.at[s], rcf.at[s], s1f.at[s], r1f.at[s], s2f.at[s], r2f.at[s], s3f.at[s], r3f.at[s])
        if s:
            table["o3", s] = lambda s=s: (s3o.at[s - 1], r3o.at[s - 1], ZP[s])
    groups["o"] = (go, rco, s1o, r1o, s2o, r2o, s3w, r3w)
    for p in range(PAIRS):
        if p < PAIRS - 1:
            gq = gf.at[p, :, :, :, pl.ds(0, 64), pl.ds(0, 384)]
            rcq = rcf.at[p, :, :, pl.ds(0, 64), pl.ds(0, 384)]
        else:
            gq, rcq = glast, rclast
        groups["q", p] = (gq, rcq, s1q.at[p], r1q.at[p], s2q.at[p], r2q.at[p], s3q.at[p], r3q.at[p])
        if p < PAIRS - 1:
            table["kv", p] = lambda p=p: (dkv.at[p % 2, :, :, pl.ds(512, 512)], rkv.at[p % 2], SB)
        else:
            for j in range(2):
                table["kv", p, j] = lambda p=p, j=j: (
                    dkv.at[p % 2, :, pl.ds(j * 64, 64), pl.ds(512, 512)],
                    rkv.at[p % 2, :, pl.ds(j * 64, 64)],
                    SB,
                )
    for g, (grad, rc, s1, r1, s2, r2, s3, r3) in groups.items():
        table["c", g] = lambda grad=grad, rc=rc: (grad.at[:, :, cc], rc, SB)
        if g in LAST:
            for i, dev in enumerate((XP, YP, DP)):
                table["d1", g, i] = lambda i=i, dev=dev, at=LAST.index(g): (s1d.at[at, i], r1d.at[at, i], dev)
            for k in (1, 2, 3):
                table["z3", g, k] = lambda s3=s3, r3=r3, k=k: (s3.at[k - 1], r3.at[k - 1], ZP[k])
            continue
        table["a1", g] = lambda s1=s1, r1=r1: (s1.at[0], r1.at[0], XP)
        table["b1", g] = lambda s1=s1, r1=r1: (s1.at[1], r1.at[1], YP)
        table["a2", g] = lambda s2=s2, r2=r2: (s2.at[0], r2.at[0], YP)
        table["b2", g] = lambda s2=s2, r2=r2: (s2.at[1], r2.at[1], XP)
        for k in (1, 2, 3):
            table["z3", g, k] = lambda s3=s3, r3=r3, k=k: (s3.at[k - 1], r3.at[k - 1], ZP[k])
    table["bc"] = lambda: (bb.at[0], rb.at[0], SB)
    for i, dev in enumerate((XP, YP, DP)):
        table["bp", i] = lambda i=i, dev=dev: (bb.at[1], rb.at[1 + i], dev)
    for k in (1, 2, 3):
        table["bz", k] = lambda k=k: (bb.at[2], rb.at[3 + k], ZP[k])
    for place, key in enumerate(table):
        ids[key] = place

    def cp(*key):
        key = key if len(key) > 1 else key[0]
        src, dst, dev = table[key]()
        place = ids[key]
        return pltpu.make_async_remote_copy(
            src_ref=src,
            dst_ref=dst,
            send_sem=send_sem.at[place],
            recv_sem=recv_sem.at[place],
            device_id=dev,
            device_id_type=MESH,
        )

    def natural(ref, firsts, columns):
        parts = [
            ref[:, :, :, pl.ds(pl.multiple_of(firsts(lax.rem(z + 4 - other, 4)), 16), 16), columns]
            for other in range(4)
        ]
        return jnp.concatenate([part.reshape(128, part.shape[-1]) for part in parts], axis=0)

    def attention_block(k):
        return k * 16

    def inner_block(k):
        return jnp.where(k == 0, 0, k * 16 + 64)

    def start(*key):
        cp(*key).start()

    def recv(*key):
        cp(*key).wait_recv()

    local = (
        [(tok, xrow.at[pl.ds(0, 512)]), (cot, cotv), (wout, wf.at[0, y, x, c, pl.ds(16, 64)])]
        + [(win.at[:, cols(zs[s])], wf.at[s, y, x, c, pl.ds(0, 16)]) for s in range(STEPS)]
        + [
            (
                ref.at[:, pl.ds(p * 128, 128)],
                (wq[p] if i < 3 or p else wq_last).at[
                    y, x, c, pl.ds(0, 16), pl.ds(i * 128 if i < 3 or p else 512, 128)
                ],
            )
            for p in range(PAIRS)
            for i, ref in enumerate((wquery, wkey, wvalue, wout_proj))
        ]
    )
    local = [pltpu.make_async_copy(src, dst, local_sem.at[i]) for i, (src, dst) in enumerate(local)]
    for one in local[7:] + local[:7]:
        one.start()
    barrier = pltpu.get_barrier_semaphore()
    peers = (XP, YP, DP, ZP[1], ZP[2], ZP[3], SB)
    for dev in peers:
        pl.semaphore_signal(barrier, inc=1, device_id=dev, device_id_type=MESH)

    own_bias = jnp.zeros((16, 128), F32)
    for offset, ref in ((0, bias_q), (16, bias_v), (32, bias_o), (48, bias_out), (64, bias_in)):
        count = ref.shape[0]
        row = jnp.broadcast_to(ref[...].astype(F32).reshape(1, count), (16, count))
        row = jnp.where(lax.broadcasted_iota(jnp.int32, (16, count), 0) == 0, row, 0.0).astype(BF)
        spot = lax.broadcasted_iota(jnp.int32, (count, 128), 0) + offset
        spread = lax.broadcasted_iota(jnp.int32, (count, 128), 1) == spot
        own_bias = own_bias + dot(row, spread.astype(F32).astype(BF), 1, 0)
    wq[0][y, x, c, pl.ds(0, 16), pl.ds(384, 128)] = own_bias.astype(BF)
    for one in local[7:]:
        one.wait()
    pl.semaphore_wait(barrier, len(peers))

    def send_z(g):
        for k in (1, 2, 3):
            start("z", g, k)
        if g[0] == "f" and g[1]:
            start("zo", g)

    def neighbours(g):
        return ("x", "y", "d") if g == ("q", 0) else ("x", "y")

    def send_early(g):
        for name in neighbours(g):
            start(name, g, 0)

    def send_plane(g):
        for k in (1, 2, 3):
            recv("z", g, k)
        if g[0] == "f" and g[1]:
            recv("zo", g)
        for name in neighbours(g):
            start(name, g, 1)

    def send_relay(g):
        for name in ("x", "y"):
            recv(name, g, 0)
            recv(name, g, 1)
            if g != ("q", 0):
                start("r" + name, g)
            if name == "x":
                start("s", g, 0)

    def send_across(g):
        if g == ("q", 0):
            recv("d", g, 0)
            recv("d", g, 1)
        else:
            recv("rx", g)
            recv("ry", g)
        start("s", g, 1)

    def all_here(g):
        recv("s", g, 0)
        recv("s", g, 1)

    Q, F = [("q", p) for p in range(PAIRS)], [("f", s) for s in range(STEPS)]
    send_z(Q[0])
    send_early(Q[0])
    local[0].wait()
    start("tok")
    send_z(Q[1])
    for p in (1, 2, 3):
        send_early(Q[p])
    for one in local[2:7]:
        one.wait()
    for s in range(STEPS):
        send_early(F[s])

    kind = lax.broadcasted_iota(jnp.int32, (16, 512), 0)
    at_own = lax.broadcasted_iota(jnp.int32, (16, 512), 1) + c * 512
    at_sib = lax.broadcasted_iota(jnp.int32, (16, 512), 1) + cc * 512
    own_seg = seg[:, pl.ds(pl.multiple_of(c * 512, 512), 512)]
    sib_seg = seg[:, pl.ds(pl.multiple_of(cc * 512, 512), 512)]
    used = fill[0]
    for half, (segs, spot) in enumerate(((own_seg, at_own), (sib_seg, at_sib))):
        unused = jnp.where(spot >= used, 1.0, 0.0)
        marks = jnp.where(kind == 8, unused, jnp.where(kind == segs, 1.0, 0.0)).astype(BF)
        for head in range(HEADS):
            kt[head, 64:80, half * 512 : half * 512 + 512] = marks
    barred = jnp.where((kind == own_seg) | (kind > 8), 0.0, -1e30).astype(BF)
    for head in range(HEADS):
        qt[head, 64:80] = barred

    gate_attn = gates[0]
    gate_feed = gates[1]
    local[1].wait()
    upstream = cotv[...].astype(F32)
    gffn[...] = (gate_feed * upstream).astype(BF)

    def take(name):
        kind, g = name[0], ({"q": "q", "f": "f", "Q": "q", "F": "f"}.get(name[1]), int(name[2:] or 0))
        if name[1] == "O":
            g = "o"
        if name in done:
            raise ValueError(name)
        done.append(name)
        if kind == "z":
            send_z(g)
        elif kind == "1":
            send_plane(g)
        elif kind == "2":
            send_relay(g)
        elif kind == "3":
            send_across(g)
        elif kind == "F":
            fold_plane(g) if g in LAST else fold_first(g)
        elif kind == "S":
            fold_second(g)
        elif g in LAST:
            fold_column(g)
        elif g == "o":
            fold_third(g)
            go_o[...] = ksum[rows(z), :]
        elif g[0] == "f":
            ffn_third(g[1])
        else:
            q_third(g[1])

    done = []

    def at_point(name):
        for one in PLAN.get(name, ()):
            take(one)

    at_point("start")
    recv("tok")
    all_here(Q[0])

    held = natural(wq[0], attention_block, slice(384, 512)).reshape(32, 16, 128)
    biasb[...] = jnp.sum(held.astype(F32), axis=1).astype(BF)

    def bias_row(offset, per, width):
        lane = lax.broadcasted_iota(jnp.int32, (128, width), 0)
        at = lax.broadcasted_iota(jnp.int32, (128, width), 1)
        pick = (lane == offset + (at & (per - 1))).astype(F32).astype(BF)
        spread = dot(biasb[...], pick, 1, 0)
        owner = lax.broadcasted_iota(jnp.int32, (32, width), 0)
        at = lax.broadcasted_iota(jnp.int32, (32, width), 1)
        return jnp.sum(jnp.where(owner == lax.shift_right_logical(at, per.bit_length() - 1), spread, 0.0), axis=0, keepdims=True)

    first_row = lax.broadcasted_iota(jnp.int32, (16, 512), 0) == 0
    ones_row = jnp.where(first_row, 1.0, 0.0).astype(BF)

    def as_rank_one(row):
        return jnp.where(first_row, jnp.broadcast_to(row, (16, 512)), 0.0).astype(BF)

    bias_q = as_rank_one(bias_row(0, 16, 512))
    bias_v = as_rank_one(bias_row(16, 16, 512))

    def project(p):
        weights = natural(wq[p], attention_block, slice(0, 384))
        ours = dot(weights, xrow[0:512], 0, 1)
        theirs = dot(weights[:, 128:384], xrow[512:1024], 0, 1)
        at = slice(p * 128, p * 128 + 128)
        grown = ours[0:128] + dot(bias_q[:, at], ones_row, 0, 0)
        grown = (grown.astype(BF).astype(F32) * 0.125).astype(BF)
        add_v = dot(bias_v[:, at], ones_row, 0, 0)
        for j in range(2):
            part = slice(j * 64, j * 64 + 64)
            qt[p * 2 + j, 0:64] = grown[part]
            kt[p * 2 + j, 0:64, 0:512] = ours[128 + j * 64 : 192 + j * 64].astype(BF)
            kt[p * 2 + j, 0:64, 512:1024] = theirs[part].astype(BF)
        vt[at, 0:512] = (ours[256:384] + add_v).astype(BF)
        vt[at, 512:1024] = (theirs[128:256] + add_v).astype(BF)

    def half_of(unit):
        return unit // 2, slice(unit % 2 * 256, unit % 2 * 256 + 256)

    def scores_of(unit):
        head, lanes = half_of(unit)
        raw = dot(kt[head], qt[head, :, lanes], 0, 0)
        own = kt[head, 0:64, lanes].astype(F32) * qt[head, 0:64, lanes].astype(F32)
        own = jnp.sum(own, axis=0, keepdims=True)
        highest = jnp.full((8, 256), -jnp.inf, F32)
        for b in range(8):
            r = slice(b * 128, b * 128 + 128)
            block = raw[r]
            if b // 2 == unit % 2 and b < 4:
                diagonal = lax.broadcasted_iota(jnp.int32, (128, 256), 1) == (
                    lax.broadcasted_iota(jnp.int32, (128, 256), 0) + b % 2 * 128
                )
                block = jnp.where(diagonal, own, block)
            st[r, lanes] = block
            highest = jnp.maximum(highest, jnp.max(block.reshape(16, 8, 256), axis=0))
        return jnp.max(highest, axis=0, keepdims=True)

    def attend(unit, highest):
        head, lanes = half_of(unit)
        total = jnp.zeros((8, 256), F32)
        for b in range(8):
            r = slice(b * 128, b * 128 + 128)
            expo = jnp.exp(st[r, lanes] - highest)
            probs[head, r, lanes] = expo
            total = total + jnp.sum(expo.reshape(16, 8, 256), axis=0)
        scale = 1.0 / jnp.sum(total, axis=0, keepdims=True)
        scales[head, :, lanes] = jnp.broadcast_to(scale, (8, 256))
        for b in range(8):
            r = slice(b * 128, b * 128 + 128)
            pb[r, lanes] = (probs[head, r, lanes] * scale).astype(BF)
        at = slice(head * 64, head * 64 + 64)
        mixt[at, lanes] = dot(vt[at], pb[:, lanes], 1, 0).astype(BF)

    for head in range(HEADS):
        first = head * 2
        if head % 2 == 0:
            if head:
                at_point("proj%d" % (head // 2))
                all_here(Q[head // 2])
            project(head // 2)
        at_point("fwd%d" % head)
        if head % 2 == 0:
            highest = scores_of(first)
        later = scores_of(first + 1)
        attend(first, highest)
        if head % 2 == 0:
            highest = scores_of(first + 2)
        attend(first + 1, later)

    at_point("outproj")
    out_weight = jnp.concatenate(
        [natural(wq_last, attention_block, slice(512, 640))] + [natural(wq[p], attention_block, slice(384, 512)) for p in (1, 2, 3)], axis=1
    )
    attn[...] = dot(mixt[...], out_weight, 0, 0) + bias_row(32, 16, 512)
    resid = xrow[0:512].astype(F32) + gate_attn * attn[...]
    rlow[...] = resid.astype(BF)
    ffn[...] = jnp.zeros((512, 512), F32)
    gres[...] = cotv[...].astype(F32)

    def fold_first(g):
        grad, rc, s1 = groups[g][:3]
        half = rc.shape[2] // 2
        recv("c", g)
        for i in range(2):
            s1[0, i] = (grad[i, xx, c, 0:half] + rc[i, xx, 0:half]).astype(BF)
            s1[1, i] = (grad[yy, i, c, half : 2 * half] + rc[yy, i, half : 2 * half]).astype(BF)
        start("a1", g)
        start("b1", g)

    def fold_second(g):
        grad, rc, s1, r1, s2, r2 = groups[g][:6]
        half = rc.shape[2] // 2
        recv("a1", g)
        s2[0] = (grad[yy, x, c, 0:half] + rc[yy, x, 0:half] + r1[0, yy].astype(F32)).astype(BF)
        start("a2", g)
        recv("b1", g)
        s2[1] = (
            grad[y, xx, c, half : 2 * half] + rc[y, xx, half : 2 * half] + r1[1, xx].astype(F32)
        ).astype(BF)
        start("b2", g)

    def fold_third(g):
        grad, rc, s1, r1, s2, r2, s3, r3 = groups[g]
        half = rc.shape[2] // 2
        width = rc.shape[3]
        recv("a2", g)
        upper = grad[y, x, c, 0:half] + rc[y, x, 0:half] + r1[0, y].astype(F32) + r2[0].astype(F32)
        ksum[0:half, 0:width] = upper
        recv("b2", g)
        lower = (
            grad[y, x, c, half : 2 * half]
            + rc[y, x, half : 2 * half]
            + r1[1, x].astype(F32)
            + r2[1].astype(F32)
        )
        ksum[half : 2 * half, 0:width] = lower
        for k in (1, 2, 3):
            s3[k - 1] = ksum[rows(zs[k]), 0:width].astype(BF)
            start("z3", g, k)

    def ffn_third(s):
        fold_third(("f", s))
        gi_o[:, cols(zs[s])] = ksum[rows(z), :]
        if s:
            s3o[s - 1] = ksum[64:128].astype(BF)
            start("o3", s)
        else:
            gout_o[...] = ksum[64:128]

    def small(row, value):
        bb[0, row : row + 1, 0:512] = value

    bb[0, :, 512:640] = jnp.zeros((8, 128), F32)

    def ffn_step(s):
        all_here(F[s])
        inner = natural(wf.at[s], inner_block, slice(0, 512))
        outer = wf[s, :, :, :, 16:80].reshape(512, 512)
        hid[...] = dot(rlow[...], inner, 1, 0) + chunk_bias[s]
        gac[...] = dot(gffn[...], outer, 1, 1)
        for b in range(8):
            r = slice(b * 64, b * 64 + 64)
            value, slope = gelu_parts(hid[r])
            act[r] = value.astype(BF)
            ghid[r] = (gac[r] * slope).astype(BF)
        ffn[...] += dot(act[...], outer, 1, 0)
        gf[s, :, :, :, 64:128] = dot(act[...], gffn[...], 0, 0).reshape(2, 2, 2, 64, 512)
        gf[s, :, :, :, 0:64] = by_chip(dot(rlow[...], ghid[...], 0, 0))
        start("c", ("f", s))
        gres[...] += dot(ghid[...], inner, 1, 1)
        sums = col_sums(ghid[...])[0:1]
        for row in range(4):
            bb[0, 4 + row : 5 + row, 0:512] = jnp.where(
                zs[s] == row, sums, bb[0, 4 + row : 5 + row, 0:512]
            )

    inner_bias = bias_row(64, 64, 2048)
    parts = [inner_bias[:, i * 512 : i * 512 + 512] for i in range(4)]
    chunk_bias = []
    for s in range(STEPS):
        picked = parts[3]
        for i in range(3):
            picked = jnp.where(zs[s] == i, parts[i], picked)
        chunk_bias.append(picked)
    for row in range(4):
        small(4 + row, jnp.zeros((1, 512), F32))

    for s in range(STEPS):
        at_point("ffn%d" % s)
        ffn_step(s)
    at_point("pre")

    waited = set()
    for key in table:
        if key[0] in ("x", "y", "rx", "ry", "s") and key[1][0] == "f":
            cp(*key).wait_send()
            waited.add(key)

    small(3, col_sums(gffn[...])[0:1])
    gattn = (gate_attn * gres[...]).astype(BF)
    small(2, col_sums(gattn)[0:1])
    go[...] = by_chip(dot(mixt[...], gattn, 1, 0))
    start("c", "o")
    gmixt[...] = dot(out_weight, gattn, 1, 1).astype(BF)
    def finish_layer():
        ffn[...] += bias_row(48, 16, 512)
        upstream = cotv[...].astype(F32)
        resid = xrow[0:512].astype(F32) + gate_attn * attn[...]
        rlow[...] = (resid + gate_feed * ffn[...]).astype(BF)
        layer_out = pltpu.make_async_copy(rlow, layer_o, local_sem.at[0])
        layer_out.start()
        feed_part = jnp.sum(jnp.sum(upstream * ffn[...], axis=0, keepdims=True), axis=1, keepdims=True)
        bb[0, 1:2, 512:640] = jnp.broadcast_to(feed_part, (1, 128))
        attn_part = jnp.sum(jnp.sum(gres[...] * attn[...], axis=0, keepdims=True), axis=1, keepdims=True)
        bb[0, 0:1, 512:640] = jnp.broadcast_to(attn_part, (1, 128))
        return layer_out


    def scores_back(unit):
        head, lanes = half_of(unit)
        at = slice(head * 64, head * 64 + 64)
        raw = dot(vt[at], gmixt[at, lanes], 0, 0)
        total = jnp.zeros((8, 256), F32)
        for b in range(8):
            r = slice(b * 128, b * 128 + 128)
            block = raw[r]
            st[r, lanes] = block
            total = total + jnp.sum((probs[head, r, lanes] * block).reshape(16, 8, 256), axis=0)
        return jnp.sum(total, axis=0, keepdims=True) * scales[head, 0:1, lanes]

    def slopes_of(unit, inner):
        head, lanes = half_of(unit)
        scale = scales[head, 0:1, lanes]
        slot = head % 2 * 2
        for b in range(8):
            r = slice(b * 128, b * 128 + 128)
            prob = probs[head, r, lanes] * scale
            place = (b // 4, b // 2 % 2, b % 2, slice(None), lanes)
            wf[(slot, *place)] = prob.astype(BF)
            wf[(slot + 1, *place)] = (prob * (st[r, lanes] - inner)).astype(BF)

    def products_of(head):
        at = slice(head * 64, head * 64 + 64)
        slot = head % 2 * 2
        prob, slope = (wf[i].reshape(1024, 512) for i in (slot, slot + 1))
        place = (head // 2 % 2, slice(None), slice(head % 2 * 64, head % 2 * 64 + 64))
        dkv[place[0], 0, place[2]] = dot(qt[head, 0:64], slope, 1, 1)
        dkv[place[0], 1, place[2]] = dot(gmixt[at], prob, 1, 1)
        if head >= 6:
            assert "FQ1" in done
            start("kv", 3, head - 6)
        dqt[at] = (dot(kt[head, 0:64], slope, 1, 0) * 0.125).astype(BF)

    def finish_pair(p):
        slot = p % 2
        at = slice(p * 128, p * 128 + 128)
        if p < PAIRS - 1:
            recv("kv", p)
        else:
            recv("kv", p, 0)
            recv("kv", p, 1)
        vt[at, 0:512] = (dkv[slot, 0, :, 0:512] + rkv[slot, 0]).astype(BF)
        vt[at, 512:1024] = (dkv[slot, 1, :, 0:512] + rkv[slot, 1]).astype(BF)
        both = jnp.concatenate([dqt[at], vt[at, 0:512], vt[at, 512:1024]], axis=0)
        if p < PAIRS - 1:
            cp("c", F[p]).wait_send()
            gf[p, :, :, :, 0:64, 0:384] = by_chip(dot(xrow[0:512], both, 0, 1))
        else:
            glast[...] = by_chip(dot(xrow[0:512], both, 0, 1))
        start("c", Q[p])
        sums = dot(jnp.ones((8, 512), BF), both, 1, 1)
        bb[0, 0:1, at] = sums[0:1, 0:128]
        bb[0, 1:2, at] = sums[0:1, 256:384]

    def token_part(p):
        at = slice(p * 128, p * 128 + 128)
        both = jnp.concatenate([dqt[at], vt[at, 0:512], vt[at, 512:1024]], axis=0)
        gres[...] += dot(both, natural(wq[p], attention_block, slice(0, 384)), 0, 1)

    def fold_plane(g):
        grad, rc = groups[g][:2]
        recv("c", g)
        for i, (yi, xi) in enumerate(((y, xx), (yy, x), (yy, xx))):
            s1d[LAST.index(g), i] = (grad[yi, xi, c] + rc[yi, xi]).astype(BF)
            start("d1", g, i)

    def fold_column(g):
        grad, rc, s3 = groups[g][0], groups[g][1], groups[g][6]
        for i in range(3):
            recv("d1", g, i)
        come = r1d.at[LAST.index(g)]
        ksum[0:64, 0:384] = (
            grad[y, x, c] + rc[y, x] + (come[0].astype(F32) + come[1].astype(F32) + come[2].astype(F32))
        )
        for k in (1, 2, 3):
            s3[k - 1] = ksum[rows(zs[k]), 0:384].astype(BF)
            start("z3", g, k)
        keep_pair(g[1])

    def q_third(p):
        fold_third(Q[p])
        keep_pair(p)

    def keep_pair(p):
        at = slice(p * 128, p * 128 + 128)
        gq_o[:, at] = ksum[rows(z), 0:128]
        gk_o[:, at] = ksum[rows(z), 128:256]
        gv_o[:, at] = ksum[rows(z), 256:384]

    inner = scores_back(0)
    for head in range(HEADS):
        at_point("bwd%d" % head)
        if head in (5, 7):
            cp("kv", (head - 5) // 2).wait_send()
        if head:
            products_of(head - 1)
        if head in (2, 4, 6):
            p = head // 2 - 1
            assert "TF%d" % p in done and (p < 2 or "FQ%d" % (p - 2) in done)
            start("kv", p)
        later = scores_back(head * 2 + 1)
        slopes_of(head * 2, inner)
        if head < HEADS - 1:
            inner = scores_back(head * 2 + 2)
        slopes_of(head * 2 + 1, later)
        if head in (3, 5, 7):
            p = head // 2 - 1
            at_point("fin%d" % p)
            finish_pair(p)
    at_point("prod7")
    products_of(HEADS - 1)
    at_point("layer")
    layer_out = finish_layer()
    at_point("fin3")
    finish_pair(3)

    start("bc")
    at_point("tok3")
    fold_plane(Q[3])
    recv("bc")
    bb[1] = bb[0] + rb[0]
    for i in range(3):
        start("bp", i)
    at_point("tok")
    for p in range(PAIRS):
        token_part(p)
    tg_out = pltpu.make_async_copy(gres, tg_o, local_sem.at[1])
    tg_out.start()

    def q_last(p):
        at = slice(p * 128, p * 128 + 128)
        for k in (1, 2, 3):
            recv("z3", ("q", p), k)
        more = r3q[p, 0].astype(F32) + r3q[p, 1].astype(F32) + r3q[p, 2].astype(F32)
        gq_o[:, at] += more[:, 0:128]
        gk_o[:, at] += more[:, 128:256]
        gv_o[:, at] += more[:, 256:384]

    at_point("last1")
    fold_column(Q[3])
    at_point("last2")
    for i in range(3):
        recv("bp", i)
    bb[2] = bb[1] + (rb[1] + rb[2] + rb[3])
    for k in (1, 2, 3):
        start("bz", k)
    assert len(done) == 53

    for s in range(STEPS):
        for k in (1, 2, 3):
            recv("z3", ("f", s), k)
    for s in range(STEPS):
        more = r3f[(s + 1) % 4, 0].astype(F32)
        for k in (2, 3):
            more = more + r3f[(s + k) % 4, k - 1].astype(F32)
        gi_o[:, cols(zs[s])] += more
    for s in (1, 2, 3):
        recv("o3", s)
        gout_o[...] += r3o[s - 1].astype(F32)
    for k in (1, 2, 3):
        recv("z3", "o", k)
        go_o[...] += r3w[k - 1].astype(F32)
    for p in range(PAIRS):
        q_last(p)
    for k in (1, 2, 3):
        recv("bz", k)
    total = bb[2] + rb[4] + rb[5] + rb[6]
    device = lo * 2 + c
    narrow = pltpu.roll(total[:, 0:512], lax.rem(512 - device * 16, 512), 1)
    wide = pltpu.roll(total[:, 0:512], lax.rem(512 - lax.rem(device, 8) * 64, 512), 1)
    owner = lax.broadcasted_iota(jnp.int32, (8, 128), 0) == 4 + lax.div(device, 8)
    small_o[0:4] = narrow[0:4, 0:128]
    small_o[4:5] = jnp.sum(jnp.where(owner, wide[:, 0:128], 0.0), axis=0, keepdims=True)
    lane = lax.broadcasted_iota(jnp.int32, (1, 128), 1)
    small_o[5:6] = jnp.where(lane == 0, total[0:1, 512:640], total[1:2, 512:640])
    small_o[6:8] = jnp.zeros((2, 128), F32)

    layer_out.wait()
    tg_out.wait()
    waited |= {("kv", 0), ("kv", 1)} | {("c", F[p]) for p in range(PAIRS - 1)}
    for key in table:
        if key not in waited:
            (cp(*key) if isinstance(key, tuple) else cp(key)).wait_send()


def results_kernel(*refs):
    taken, small, given, held, sem = refs[:8], refs[8], refs[9:23], refs[23:31], refs[31]
    steps = []
    for i in range(8):
        there = given[i].at[0] if i < 2 else given[i]
        steps.append(
            (
                pltpu.make_async_copy(taken[i], held[i], sem.at[i]),
                pltpu.make_async_copy(held[i], there, sem.at[8 + i]),
            )
        )
    for come, _ in steps:
        come.start()
    for row, ref in enumerate(given[8:]):
        ref[...] = small[row, 0 : ref.shape[0]]
    for come, go in steps:
        come.wait()
        go.start()
    for _, go in steps:
        go.wait()


def scratch():
    v = pltpu.VMEM
    return [
        v((1024, 512), BF),
        v((512, 512), BF),
        v((3, 2, 2, 2, 64, 512), BF),
        v((2, 2, 2, 64, 640), BF),
        v((4, 2, 2, 2, 128, 512), BF),
        v((8, 80, 512), BF),
        v((8, 80, 1024), BF),
        v((512, 1024), BF),
        v((8, 1024, 512), F32),
        v((8, 8, 512), F32),
        v((1024, 512), F32),
        v((1024, 512), BF),
        v((512, 512), BF),
        v((512, 512), F32),
        v((512, 512), BF),
        v((512, 512), F32),
        v((512, 512), F32),
        v((512, 512), BF),
        v((512, 512), BF),
        v((512, 512), BF),
        v((2, 2, 128, 1024), F32),
        v((2, 2, 128, 512), F32),
        v((4, 2, 2, 2, 128, 512), F32),
        v((4, 2, 2, 128, 512), F32),
        v((4, 2, 2, 64, 512), BF),
        v((4, 2, 2, 64, 512), BF),
        v((4, 2, 64, 512), BF),
        v((4, 2, 64, 512), BF),
        v((4, 3, 16, 512), BF),
        v((4, 3, 16, 512), BF),
        v((3, 64, 512), BF),
        v((3, 64, 512), BF),
        v((2, 2, 2, 64, 512), F32),
        v((2, 2, 64, 512), F32),
        v((2, 2, 32, 512), BF),
        v((2, 2, 32, 512), BF),
        v((2, 32, 512), BF),
        v((2, 32, 512), BF),
        v((3, 16, 512), BF),
        v((3, 16, 512), BF),
        v((4, 2, 2, 32, 384), BF),
        v((4, 2, 2, 32, 384), BF),
        v((4, 2, 32, 384), BF),
        v((4, 2, 32, 384), BF),
        v((4, 3, 16, 384), BF),
        v((4, 3, 16, 384), BF),
        v((2, 2, 2, 64, 384), F32),
        v((2, 2, 64, 384), F32),
        v((2, 3, 64, 384), BF),
        v((2, 3, 64, 384), BF),
        v((128, 512), F32),
        v((3, 8, 640), F32),
        v((7, 8, 640), F32),
        v((32, 128), BF),
        pltpu.SemaphoreType.DMA((256,)),
        pltpu.SemaphoreType.DMA((256,)),
        pltpu.SemaphoreType.DMA((24,)),
    ]


def on_device(
    tokens,
    segments,
    fill_length,
    query_weight,
    key_weight,
    value_weight,
    output_weight,
    query_bias,
    value_bias,
    output_bias,
    inner_weight,
    inner_bias,
    outer_weight,
    outer_bias,
    residual_gates,
    cotangent,
):
    names = ("dp", "shard")
    several = lax.axis_size("dp") > GROUP
    place = lax.rem(lax.axis_index("dp"), GROUP) * 2 + lax.axis_index("shard")

    def block_of(shard):
        if not several:
            return shard
        whole = lax.all_gather(shard, names, axis=0, tiled=True)
        rows = whole.shape[0] // (2 * GROUP)
        return lax.dynamic_slice_in_dim(whole, place * rows, rows, 0)

    def owned(block):
        if not several:
            return block
        rows = block.shape[0]
        whole = jnp.zeros((rows * 2 * GROUP, *block.shape[1:]), F32)
        whole = lax.dynamic_update_slice_in_dim(whole, block, place * rows, 0)
        return lax.psum_scatter(whole, names, scatter_dimension=0, tiled=True)

    query_weight, key_weight, value_weight, output_weight, inner_weight, outer_weight = map(
        block_of, (query_weight, key_weight, value_weight, output_weight, inner_weight, outer_weight)
    )
    query_bias, value_bias, output_bias, inner_bias, outer_bias = map(
        block_of, (query_bias, value_bias, output_bias, inner_bias, outer_bias)
    )
    vmem = pl.BlockSpec(memory_space=pltpu.VMEM)
    smem = pl.BlockSpec(memory_space=pltpu.SMEM)
    hbm = pl.BlockSpec(memory_space=pl.ANY)
    shape = jax.ShapeDtypeStruct
    outs = pl.pallas_call(
        layer_kernel,
        out_shape=[
            shape((512, 512), BF),
            shape((512, 512), F32),
            shape((16, 512), F32),
            shape((16, 512), F32),
            shape((16, 512), F32),
            shape((16, 512), F32),
            shape((16, 2048), F32),
            shape((64, 512), F32),
            shape((8, 128), F32),
        ],
        in_specs=[hbm, hbm, vmem, smem, smem] + [vmem] * 5 + [hbm] * 6,
        out_specs=[hbm, hbm] + [vmem] * 7,
        scratch_shapes=scratch(),
        compiler_params=pltpu.CompilerParams(
            collective_id=0, has_side_effects=True, vmem_limit_bytes=VMEM_BYTES
        ),
    )(
        tokens.reshape(512, 512),
        cotangent.reshape(512, 512),
        segments,
        fill_length,
        residual_gates,
        query_bias,
        value_bias,
        output_bias,
        outer_bias,
        inner_bias,
        query_weight,
        key_weight,
        value_weight,
        output_weight,
        inner_weight,
        outer_weight,
    )
    flat = [shape(o.shape, o.dtype) for o in outs[2:8]] + [shape((n,), F32) for n in (16, 16, 16, 16, 64, 2)]
    outs = pl.pallas_call(
        results_kernel,
        out_shape=[shape((1, 512, 512), BF), shape((1, 512, 512), F32)] + flat,
        in_specs=[pl.BlockSpec(memory_space=pltpu.HBM)] * 8 + [vmem],
        out_specs=[hbm] * 8 + [vmem] * 6,
        scratch_shapes=[pltpu.VMEM(o.shape, o.dtype) for o in outs[:8]] + [pltpu.SemaphoreType.DMA((16,))],
        compiler_params=pltpu.CompilerParams(vmem_limit_bytes=VMEM_BYTES),
    )(*outs)
    layer, token_grads, gq, gk, gv, go, gi, gout, g_query, g_value, g_output, g_outer, g_inner, gate_sums = outs
    if several:
        gate_sums = lax.psum(jnp.where(place == 0, gate_sums, 0.0), names)
    grads = (gq, gk, gv, go, g_query, g_value, g_output, gi, g_inner, gout, g_outer)
    return (layer, token_grads, *map(owned, grads), gate_sums)


def solution(mesh):
    spread = P(("dp", "shard"))
    return jax.shard_map(
        on_device,
        mesh=mesh,
        in_specs=(
            P("dp", "shard", None),
            P("dp", None),
            P("dp"),
            *([P(("dp", "shard"), None)] * 4),
            *([spread] * 3),
            P(("dp", "shard"), None),
            spread,
            P(("dp", "shard"), None),
            spread,
            P(),
            P("dp", "shard", None),
        ),
        out_specs=(
            P("dp", "shard", None),
            P("dp", "shard", None),
            *([P(("dp", "shard"), None)] * 4),
            *([spread] * 3),
            P(("dp", "shard"), None),
            spread,
            P(("dp", "shard"), None),
            spread,
            P(),
        ),
        check_vma=False,
    )
```

time: 119 us -> 90.7 us (0.76)
  local copies, waits for them, and re-layouts: 14.7 us -> 0 us
  Pallas kernels: 102 us -> 89 us
    pallas_call x1, Pallas kernels: 102 us -> 85.1 us  [on_device(): pl.pallas_call(layer_kernel, out_shape=[shape((512, 512), BF), shape((512...]
    unnamed x52 -> x0, local copies, waits for them, and re-layouts: 10.7 us -> none
    pallas_call x0 -> x1, Pallas kernels: none -> 3.83 us  [on_device(): pl.pallas_call(results_kernel, out_shape=[shape((1, 512, 512), BF), shape...]
    squeeze x2 -> x0, local copies, waits for them, and re-layouts: 2.55 us -> none  [the longest x1 1.36 us: on_device(): small[3, 0:16]]
    slice x1 -> x0, local copies, waits for them, and re-layouts: 1.31 us -> none  [on_device(): gate_sums = small[5:7, 0]]
where the time goes in v2:
time: 90.7 us; the launch traced here: 90.4 us
  Pallas kernels  89 us (98%)
  between operations  1.49 us (2%)
    pallas_call x1, Pallas kernels, on_device(): pl.pallas_call(layer_kernel, out_shape=[shape((512, 512), BF), shape((512...  85.1 us
    pallas_call x1, Pallas kernels, on_device(): pl.pallas_call(results_kernel, out_shape=[shape((1, 512, 512), BF), shape...  3.83 us

profile of v2, /device:TPU:0, one launch (start us, length us, event | category | flops | bytes accessed | tf_op | source)
XLA Modules:
  0.0 90.4 jit_solution(7616333314602631673)
XLA Ops:
  1.3 85.1 %shard_map.263 = (bf16[512,512]{1,0:T(8,128)(2,1)}, f32[512,512]{1,0:T(8,128)}, f32[16,512]{1,0:T(8,128)}, f32[16,512]{1,0:T(8,128)}, f32[16,512]{1,0:T(8,128)},...) custom-call(bf16[512,512]{1,0:T(8,128)(2,1)} %bitcast.2, ...), custom_call_target="tpu_custom_call" | custom-call | tf_op jit(solution)/shard_map/pallas_call | solution.py:996
  86.4 3.8 %shard_map.264 = (bf16[1,512,512]{2,1,0:T(8,128)(2,1)}, f32[1,512,512]{2,1,0:T(8,128)}, f32[16,512]{1,0:T(8,128)}, f32[16,512]{1,0:T(8,128)}, f32[16,512]{1,0:T(...) custom-call(bf16[512,512]{1,0:T(8,128)(2,1)} %get-tuple-element.37.r, ...), custom_call_target="tpu_custom_call" | custom-call | tf_op jit(solution)/shard_map/pallas_call | solution.py:1034

commit v3 on v2

--- a/solution.py
+++ b/solution.py
@@ -13,32 +13,37 @@
 PAIRS = 4
 VMEM_BYTES = 64 * 2**20 - 2**17
 PLAN = {
-    "start": ("1q0", "zq2", "1q1", "zq3", "1q2", "zf0", "2q0", "3q0", "1q3", "zf1", "2q1",),
-    "fwd0": ("2q2", "1f0", "zf2",),
-    "fwd1": ("2q3",),
-    "proj1": ("3q1", "3q2", "1f1", "zf3", "2f0",),
-    "fwd2": ("3q3",),
-    "proj2": ("1f2",),
-    "fwd5": ("2f1",),
-    "proj3": ("3f0", "1f3",),
+    "fwd0": ("2q2",),
+    "fwd1": ("2q3", "zf3", "1f1", "3q1",),
+    "proj1": ("2f0",),
+    "fwd2": ("3q2",),
+    "fwd3": ("3q3", "1f2",),
+    "proj3": ("2f1", "1f3",),
+    "fwd6": ("3f0",),
     "outproj": ("2f2",),
-    "ffn0": ("3f1",),
+    "mid0": ("3f1",),
     "ffn1": ("2f3",),
-    "ffn2": ("3f2", "3f3", "FF0",),
+    "mid1": ("3f2",),
+    "ffn2": ("FF0", "3f3",),
     "ffn3": ("FF1",),
     "pre": ("SF0",),
     "bwd0": ("FF2",),
     "bwd1": ("SF1",),
-    "bwd2": ("TF0", "FF3",),
-    "bwd3": ("FO", "SF2",),
-    "fin0": ("TF1",),
-    "bwd5": ("SF3", "FQ0",),
-    "fin1": ("SO", "TF2",),
-    "bwd6": ("TF3",),
-    "bwd7": ("TO", "SQ0", "FQ1",),
-    "prod7": ("TQ0", "SQ1",),
-    "fin3": ("TQ1", "FQ2",),
-    "last1": ("TQ2",),
+    "bwd2": ("TF0",),
+    "bwd3": ("FF3",),
+    "fin0": ("SF2",),
+    "bwd4": ("TF1",),
+    "bwd5": ("FO",),
+    "fin1": ("FQ0",),
+    "bwd6": ("SF3", "TF2",),
+    "bwd7": ("FQ1",),
+    "fin2": ("SQ0",),
+    "prod7": ("TF3", "EP",),
+    "layer": ("SO",),
+    "fin3": ("FQ2",),
+    "tok3": ("EZ", "TQ0", "SQ1", "TO",),
+    "last1": ("TQ1", "TQ2",),
+    "start": ("zq2", "1q0", "zq3", "1q1", "zf0", "1q2", "zf1", "1q3", "zf2", "2q0", "3q0", "2q1", "1f0",),
 }
 STEPS = 4
 
@@ -74,9 +79,9 @@
 def layer_kernel(
     tok,
     cot,
-    seg,
-    fill,
-    gates,
+    seg_in,
+    fill_in,
+    gates_in,
     bias_q,
     bias_v,
     bias_o,
@@ -97,6 +102,22 @@
     gi_o,
     gout_o,
     small_o,
+    seg,
+    fill,
+    gates,
+    own_q,
+    own_v,
+    own_o,
+    own_out,
+    own_in,
+    biasf,
+    gq_s,
+    gk_s,
+    gv_s,
+    go_s,
+    gi_s,
+    gout_s,
+    small_s,
     xrow,
     cotv,
     wq_rest,
@@ -150,6 +171,8 @@
     ksum,
     bb,
     rb,
+    eb,
+    re,
     biasb,
     send_sem,
     recv_sem,
@@ -264,26 +287,82 @@
         table["b2", g] = lambda s2=s2, r2=r2: (s2.at[1], r2.at[1], XP)
         for k in (1, 2, 3):
             table["z3", g, k] = lambda s3=s3, r3=r3, k=k: (s3.at[k - 1], r3.at[k - 1], ZP[k])
-    table["bc"] = lambda: (bb.at[0], rb.at[0], SB)
-    for i, dev in enumerate((XP, YP, DP)):
-        table["bp", i] = lambda i=i, dev=dev: (bb.at[1], rb.at[1 + i], dev)
-    for k in (1, 2, 3):
-        table["bz", k] = lambda k=k: (bb.at[2], rb.at[3 + k], ZP[k])
-    for place, key in enumerate(table):
-        ids[key] = place
-
-    def cp(*key):
+    for kind, (mine, come) in {"b": (bb, rb), "e": (eb, re)}.items():
+        table[kind + "c"] = lambda mine=mine, come=come: (mine.at[0], come.at[0], SB)
+        for i, dev in enumerate((XP, YP, DP)):
+            table[kind + "p", i] = lambda i=i, dev=dev, mine=mine, come=come: (mine.at[1], come.at[1 + i], dev)
+        for k in (1, 2, 3):
+            table[kind + "z", k] = lambda k=k, mine=mine, come=come: (mine.at[2], come.at[3 + k], ZP[k])
+
+    def batch(key):
+        if not isinstance(key, tuple):
+            return key
+        kind = {"zo": "z", "rx": "r", "ry": "r", "a1": "1", "b1": "1", "a2": "2", "b2": "2"}.get(key[0], key[0])
+        if kind in ("bp", "bz", "ep", "ez", "o3"):
+            return kind
+        if kind == "z3":
+            return "z3" + key[1][0]
+        return (kind, key[1])
+
+    for key in table:
+        ids.setdefault(batch(key), len(ids))
+    weight_batches = [one for one in ids if one[0] in ("z", "x", "y", "d", "r", "s") and isinstance(one, tuple)]
+    sum_batches = [one for one in ids if one not in weight_batches and one != "tok"]
+    send_ids = {one: i for i, one in enumerate(weight_batches + ["tok"])}
+    early = [one for one in weight_batches if one[1][0] == "q"] + [one for one in weight_batches if one[1][0] == "f"]
+    late = [("kv", 2), ("kv", 3), "z3q", "bc", "bp", "bz", "ec", "ep", "ez"]
+    late += [one for one in sum_batches if isinstance(one[1], tuple) and one[1][0] == "q"]
+    for one, place in zip([one for one in sum_batches if one not in late] + late, early):
+        send_ids[one] = send_ids[place]
+    whole = {"tok": xrow.at[pl.ds(512, 512)]}
+    for g in [("q", p) for p in range(PAIRS)] + [("f", s) for s in range(STEPS)]:
+        chunk = wq[g[1]] if g[0] == "q" else wf.at[g[1]]
+        low = 80 if g == ("f", 0) else 16
+        whole["z", g] = chunk.at[y, x, c, pl.ds(low, chunk.shape[3] - low)]
+        whole["x", g] = chunk.at[y, xx, c]
+        whole["y", g] = chunk.at[yy, x, c]
+        whole["d", g] = whole["r", g] = chunk.at[yy, xx, c]
+        whole["s", g] = chunk.at[:, :, cc]
+    for g, (grad, rc, s1, r1, s2, r2, s3, r3) in groups.items():
+        whole["c", g], whole["1", g], whole["2", g] = rc, r1, r2
+    for i, g in enumerate(LAST):
+        whole["d1", g] = r1d.at[i]
+    for p in range(PAIRS):
+        whole["kv", p] = rkv.at[p % 2]
+    whole |= {"z3f": r3f, "z3q": r3q, "z3o": r3w, "o3": r3o, "bc": rb.at[0], "ec": re.at[0]}
+    whole |= {"bp": rb.at[pl.ds(1, 3)], "bz": rb.at[pl.ds(4, 3)], "ep": re.at[pl.ds(1, 3)], "ez": re.at[pl.ds(4, 3)]}
+
+    def start(*key):
         key = key if len(key) > 1 else key[0]
         src, dst, dev = table[key]()
-        place = ids[key]
-        return pltpu.make_async_remote_copy(
+        pltpu.make_async_remote_copy(
             src_ref=src,
             dst_ref=dst,
-            send_sem=send_sem.at[place],
-            recv_sem=recv_sem.at[place],
+            send_sem=send_sem.at[send_ids[batch(key)]],
+            recv_sem=recv_sem.at[ids[batch(key)]],
             device_id=dev,
             device_id_type=MESH,
+        ).start()
+
+    def all_of(one):
+        return pltpu.make_async_remote_copy(
+            src_ref=whole[one],
+            dst_ref=whole[one],
+            send_sem=send_sem.at[send_ids[one]],
+            recv_sem=recv_sem.at[ids[one]],
+            device_id=SB,
+            device_id_type=MESH,
         )
+
+    waited = set()
+
+    def recv(*key):
+        all_of(key if len(key) > 1 else key[0]).wait_recv()
+
+    def sent(*key):
+        one = key if len(key) > 1 else key[0]
+        waited.add(one)
+        all_of(one).wait_send()
 
     def natural(ref, firsts, columns):
         parts = [
@@ -297,12 +376,6 @@
 
     def inner_block(k):
         return jnp.where(k == 0, 0, k * 16 + 64)
-
-    def start(*key):
-        cp(*key).start()
-
-    def recv(*key):
-        cp(*key).wait_recv()
 
     local = (
         [(tok, xrow.at[pl.ds(0, 512)]), (cot, cotv), (wout, wf.at[0, y, x, c, pl.ds(16, 64)])]
@@ -319,23 +392,27 @@
         ]
     )
     local = [pltpu.make_async_copy(src, dst, local_sem.at[i]) for i, (src, dst) in enumerate(local)]
-    for one in local[7:] + local[:7]:
+    needed = [(bias_q, own_q), (bias_v, own_v), (bias_o, own_o), (bias_out, own_out), (bias_in, own_in)]
+    needed += [(seg_in, seg), (fill_in, fill), (gates_in, gates)]
+    needed = [pltpu.make_async_copy(src, dst, local_sem.at[len(local) + i]) for i, (src, dst) in enumerate(needed)]
+    for one in local[7:11] + needed + local[:7] + local[11:]:
         one.start()
     barrier = pltpu.get_barrier_semaphore()
     peers = (XP, YP, DP, ZP[1], ZP[2], ZP[3], SB)
     for dev in peers:
         pl.semaphore_signal(barrier, inc=1, device_id=dev, device_id_type=MESH)
 
-    own_bias = jnp.zeros((16, 128), F32)
-    for offset, ref in ((0, bias_q), (16, bias_v), (32, bias_o), (48, bias_out), (64, bias_in)):
+    biasf[...] = jnp.zeros((8, 128), F32)
+    for one in needed:
+        one.wait()
+    for row, ref in enumerate((own_q, own_v, own_o, own_out, own_in)):
         count = ref.shape[0]
-        row = jnp.broadcast_to(ref[...].astype(F32).reshape(1, count), (16, count))
-        row = jnp.where(lax.broadcasted_iota(jnp.int32, (16, count), 0) == 0, row, 0.0).astype(BF)
-        spot = lax.broadcasted_iota(jnp.int32, (count, 128), 0) + offset
-        spread = lax.broadcasted_iota(jnp.int32, (count, 128), 1) == spot
-        own_bias = own_bias + dot(row, spread.astype(F32).astype(BF), 1, 0)
+        biasf[row : row + 1, 0:count] = ref[...].astype(F32).reshape(1, count)
+    packed = jnp.sum(pltpu.roll(biasf[...], 0, 1, stride=16, stride_axis=0), axis=0, keepdims=True)
+    first = lax.broadcasted_iota(jnp.int32, (16, 128), 0) == 0
+    own_bias = jnp.where(first, jnp.broadcast_to(packed, (16, 128)), 0.0)
     wq[0][y, x, c, pl.ds(0, 16), pl.ds(384, 128)] = own_bias.astype(BF)
-    for one in local[7:]:
+    for one in local[7:11]:
         one.wait()
     pl.semaphore_wait(barrier, len(peers))
 
@@ -353,17 +430,13 @@
             start(name, g, 0)
 
     def send_plane(g):
-        for k in (1, 2, 3):
-            recv("z", g, k)
-        if g[0] == "f" and g[1]:
-            recv("zo", g)
+        recv("z", g)
         for name in neighbours(g):
             start(name, g, 1)
 
     def send_relay(g):
         for name in ("x", "y"):
-            recv(name, g, 0)
-            recv(name, g, 1)
+            recv(name, g)
             if g != ("q", 0):
                 start("r" + name, g)
             if name == "x":
@@ -371,23 +444,22 @@
 
     def send_across(g):
         if g == ("q", 0):
-            recv("d", g, 0)
-            recv("d", g, 1)
+            recv("d", g)
         else:
-            recv("rx", g)
-            recv("ry", g)
+            recv("r", g)
         start("s", g, 1)
 
     def all_here(g):
-        recv("s", g, 0)
-        recv("s", g, 1)
+        recv("s", g)
 
     Q, F = [("q", p) for p in range(PAIRS)], [("f", s) for s in range(STEPS)]
     send_z(Q[0])
     send_early(Q[0])
+    for one in local[11:]:
+        one.wait()
+    send_z(Q[1])
     local[0].wait()
     start("tok")
-    send_z(Q[1])
     for p in (1, 2, 3):
         send_early(Q[p])
     for one in local[2:7]:
@@ -416,7 +488,22 @@
     upstream = cotv[...].astype(F32)
     gffn[...] = (gate_feed * upstream).astype(BF)
 
+    def small_plane():
+        recv("ec")
+        eb[1] = eb[0] + re[0]
+        for i in range(3):
+            start("ep", i)
+
+    def small_column():
+        recv("ep")
+        eb[2] = eb[1] + (re[1] + re[2] + re[3])
+        for k in (1, 2, 3):
+            start("ez", k)
+
     def take(name):
+        if name in ("EP", "EZ"):
+            done.append(name)
+            return small_plane() if name == "EP" else small_column()
         kind, g = name[0], ({"q": "q", "f": "f", "Q": "q", "F": "f"}.get(name[1]), int(name[2:] or 0))
         if name[1] == "O":
             g = "o"
@@ -439,13 +526,18 @@
             fold_column(g)
         elif g == "o":
             fold_third(g)
-            go_o[...] = ksum[rows(z), :]
+            go_s[...] = ksum[rows(z), :]
         elif g[0] == "f":
             ffn_third(g[1])
         else:
             q_third(g[1])
 
-    done = []
+    done, given = [], []
+
+    def give(held, out):
+        one = pltpu.make_async_copy(held, out, local_sem.at[len(given)])
+        one.start()
+        given.append(one)
 
     def at_point(name):
         for one in PLAN.get(name, ()):
@@ -546,6 +638,10 @@
         attend(first + 1, later)
 
     at_point("outproj")
+    sent("tok")
+    for one in weight_batches:
+        if one[1][0] == "q":
+            sent(*one)
     out_weight = jnp.concatenate(
         [natural(wq_last, attention_block, slice(512, 640))] + [natural(wq[p], attention_block, slice(384, 512)) for p in (1, 2, 3)], axis=1
     )
@@ -568,10 +664,9 @@
     def fold_second(g):
         grad, rc, s1, r1, s2, r2 = groups[g][:6]
         half = rc.shape[2] // 2
-        recv("a1", g)
+        recv("1", g)
         s2[0] = (grad[yy, x, c, 0:half] + rc[yy, x, 0:half] + r1[0, yy].astype(F32)).astype(BF)
         start("a2", g)
-        recv("b1", g)
         s2[1] = (
             grad[y, xx, c, half : 2 * half] + rc[y, xx, half : 2 * half] + r1[1, xx].astype(F32)
         ).astype(BF)
@@ -581,10 +676,9 @@
         grad, rc, s1, r1, s2, r2, s3, r3 = groups[g]
         half = rc.shape[2] // 2
         width = rc.shape[3]
-        recv("a2", g)
+        recv("2", g)
         upper = grad[y, x, c, 0:half] + rc[y, x, 0:half] + r1[0, y].astype(F32) + r2[0].astype(F32)
         ksum[0:half, 0:width] = upper
-        recv("b2", g)
         lower = (
             grad[y, x, c, half : 2 * half]
             + rc[y, x, half : 2 * half]
@@ -598,17 +692,18 @@
 
     def ffn_third(s):
         fold_third(("f", s))
-        gi_o[:, cols(zs[s])] = ksum[rows(z), :]
+        gi_s[:, cols(zs[s])] = ksum[rows(z), :]
         if s:
             s3o[s - 1] = ksum[64:128].astype(BF)
             start("o3", s)
         else:
-            gout_o[...] = ksum[64:128]
+            gout_s[...] = ksum[64:128]
 
     def small(row, value):
-        bb[0, row : row + 1, 0:512] = value
-
-    bb[0, :, 512:640] = jnp.zeros((8, 128), F32)
+        eb[0, row : row + 1, :] = value
+
+    bb[0] = jnp.zeros((16, 128), F32)
+    eb[0] = jnp.zeros((8, 512), F32)
 
     def ffn_step(s):
         all_here(F[s])
@@ -621,6 +716,7 @@
             value, slope = gelu_parts(hid[r])
             act[r] = value.astype(BF)
             ghid[r] = (gac[r] * slope).astype(BF)
+        at_point("mid%d" % s)
         ffn[...] += dot(act[...], outer, 1, 0)
         gf[s, :, :, :, 64:128] = dot(act[...], gffn[...], 0, 0).reshape(2, 2, 2, 64, 512)
         gf[s, :, :, :, 0:64] = by_chip(dot(rlow[...], ghid[...], 0, 0))
@@ -628,9 +724,7 @@
         gres[...] += dot(ghid[...], inner, 1, 1)
         sums = col_sums(ghid[...])[0:1]
         for row in range(4):
-            bb[0, 4 + row : 5 + row, 0:512] = jnp.where(
-                zs[s] == row, sums, bb[0, 4 + row : 5 + row, 0:512]
-            )
+            eb[0, 4 + row : 5 + row, :] = jnp.where(zs[s] == row, sums, eb[0, 4 + row : 5 + row, :])
 
     inner_bias = bias_row(64, 64, 2048)
     parts = [inner_bias[:, i * 512 : i * 512 + 512] for i in range(4)]
@@ -640,23 +734,19 @@
         for i in range(3):
             picked = jnp.where(zs[s] == i, parts[i], picked)
         chunk_bias.append(picked)
-    for row in range(4):
-        small(4 + row, jnp.zeros((1, 512), F32))
-
     for s in range(STEPS):
         at_point("ffn%d" % s)
         ffn_step(s)
     at_point("pre")
 
-    waited = set()
-    for key in table:
-        if key[0] in ("x", "y", "rx", "ry", "s") and key[1][0] == "f":
-            cp(*key).wait_send()
-            waited.add(key)
-
-    small(3, col_sums(gffn[...])[0:1])
+    for one in weight_batches:
+        if one[1][0] == "f":
+            sent(*one)
+
+    small(1, col_sums(gffn[...])[0:1])
     gattn = (gate_attn * gres[...]).astype(BF)
-    small(2, col_sums(gattn)[0:1])
+    small(0, col_sums(gattn)[0:1])
+    start("ec")
     go[...] = by_chip(dot(mixt[...], gattn, 1, 0))
     start("c", "o")
     gmixt[...] = dot(out_weight, gattn, 1, 1).astype(BF)
@@ -665,13 +755,11 @@
         upstream = cotv[...].astype(F32)
         resid = xrow[0:512].astype(F32) + gate_attn * attn[...]
         rlow[...] = (resid + gate_feed * ffn[...]).astype(BF)
-        layer_out = pltpu.make_async_copy(rlow, layer_o, local_sem.at[0])
-        layer_out.start()
+        give(rlow, layer_o)
         feed_part = jnp.sum(jnp.sum(upstream * ffn[...], axis=0, keepdims=True), axis=1, keepdims=True)
-        bb[0, 1:2, 512:640] = jnp.broadcast_to(feed_part, (1, 128))
+        bb[0, 9:10] = jnp.broadcast_to(feed_part, (1, 128))
         attn_part = jnp.sum(jnp.sum(gres[...] * attn[...], axis=0, keepdims=True), axis=1, keepdims=True)
-        bb[0, 0:1, 512:640] = jnp.broadcast_to(attn_part, (1, 128))
-        return layer_out
+        bb[0, 8:9] = jnp.broadcast_to(attn_part, (1, 128))
 
 
     def scores_back(unit):
@@ -712,23 +800,19 @@
     def finish_pair(p):
         slot = p % 2
         at = slice(p * 128, p * 128 + 128)
-        if p < PAIRS - 1:
-            recv("kv", p)
-        else:
-            recv("kv", p, 0)
-            recv("kv", p, 1)
+        recv("kv", p)
         vt[at, 0:512] = (dkv[slot, 0, :, 0:512] + rkv[slot, 0]).astype(BF)
         vt[at, 512:1024] = (dkv[slot, 1, :, 0:512] + rkv[slot, 1]).astype(BF)
         both = jnp.concatenate([dqt[at], vt[at, 0:512], vt[at, 512:1024]], axis=0)
         if p < PAIRS - 1:
-            cp("c", F[p]).wait_send()
+            sent("c", F[p])
             gf[p, :, :, :, 0:64, 0:384] = by_chip(dot(xrow[0:512], both, 0, 1))
         else:
             glast[...] = by_chip(dot(xrow[0:512], both, 0, 1))
         start("c", Q[p])
         sums = dot(jnp.ones((8, 512), BF), both, 1, 1)
-        bb[0, 0:1, at] = sums[0:1, 0:128]
-        bb[0, 1:2, at] = sums[0:1, 256:384]
+        bb[0, p : p + 1] = sums[0:1, 0:128]
+        bb[0, 4 + p : 5 + p] = sums[0:1, 256:384]
 
     def token_part(p):
         at = slice(p * 128, p * 128 + 128)
@@ -744,8 +828,7 @@
 
     def fold_column(g):
         grad, rc, s3 = groups[g][0], groups[g][1], groups[g][6]
-        for i in range(3):
-            recv("d1", g, i)
+        recv("d1", g)
         come = r1d.at[LAST.index(g)]
         ksum[0:64, 0:384] = (
             grad[y, x, c] + rc[y, x] + (come[0].astype(F32) + come[1].astype(F32) + come[2].astype(F32))
@@ -761,15 +844,15 @@
 
     def keep_pair(p):
         at = slice(p * 128, p * 128 + 128)
-        gq_o[:, at] = ksum[rows(z), 0:128]
-        gk_o[:, at] = ksum[rows(z), 128:256]
-        gv_o[:, at] = ksum[rows(z), 256:384]
+        gq_s[:, at] = ksum[rows(z), 0:128]
+        gk_s[:, at] = ksum[rows(z), 128:256]
+        gv_s[:, at] = ksum[rows(z), 256:384]
 
     inner = scores_back(0)
     for head in range(HEADS):
         at_point("bwd%d" % head)
         if head in (5, 7):
-            cp("kv", (head - 5) // 2).wait_send()
+            sent("kv", (head - 5) // 2)
         if head:
             products_of(head - 1)
         if head in (2, 4, 6):
@@ -788,7 +871,7 @@
     at_point("prod7")
     products_of(HEADS - 1)
     at_point("layer")
-    layer_out = finish_layer()
+    finish_layer()
     at_point("fin3")
     finish_pair(3)
 
@@ -802,90 +885,105 @@
     at_point("tok")
     for p in range(PAIRS):
         token_part(p)
-    tg_out = pltpu.make_async_copy(gres, tg_o, local_sem.at[1])
-    tg_out.start()
+    give(gres, tg_o)
 
     def q_last(p):
         at = slice(p * 128, p * 128 + 128)
-        for k in (1, 2, 3):
-            recv("z3", ("q", p), k)
         more = r3q[p, 0].astype(F32) + r3q[p, 1].astype(F32) + r3q[p, 2].astype(F32)
-        gq_o[:, at] += more[:, 0:128]
-        gk_o[:, at] += more[:, 128:256]
-        gv_o[:, at] += more[:, 256:384]
+        gq_s[:, at] += more[:, 0:128]
+        gk_s[:, at] += more[:, 128:256]
+        gv_s[:, at] += more[:, 256:384]
 
     at_point("last1")
     fold_column(Q[3])
     at_point("last2")
-    for i in range(3):
-        recv("bp", i)
+    recv("bp")
     bb[2] = bb[1] + (rb[1] + rb[2] + rb[3])
     for k in (1, 2, 3):
         start("bz", k)
-    assert len(done) == 53
-
-    for s in range(STEPS):
-        for k in (1, 2, 3):
-            recv("z3", ("f", s), k)
+    assert len(done) == 55
+
+    recv("z3f")
     for s in range(STEPS):
         more = r3f[(s + 1) % 4, 0].astype(F32)
         for k in (2, 3):
             more = more + r3f[(s + k) % 4, k - 1].astype(F32)
-        gi_o[:, cols(zs[s])] += more
+        gi_s[:, cols(zs[s])] += more
+    give(gi_s, gi_o)
+    recv("o3")
     for s in (1, 2, 3):
-        recv("o3", s)
-        gout_o[...] += r3o[s - 1].astype(F32)
+        gout_s[...] += r3o[s - 1].astype(F32)
+    give(gout_s, gout_o)
+    recv("z3o")
     for k in (1, 2, 3):
-        recv("z3", "o", k)
-        go_o[...] += r3w[k - 1].astype(F32)
+        go_s[...] += r3w[k - 1].astype(F32)
+    give(go_s, go_o)
+    recv("z3q")
     for p in range(PAIRS):
         q_last(p)
-    for k in (1, 2, 3):
-        recv("bz", k)
+    give(gq_s, gq_o)
+    give(gk_s, gk_o)
+    give(gv_s, gv_o)
+    recv("ez")
+    total = eb[2] + re[4] + re[5] + re[6]
+    device = lo * 2 + c
+    narrow = pltpu.roll(total, lax.rem(512 - device * 16, 512), 1)
+    wide = pltpu.roll(total, lax.rem(512 - lax.rem(device, 8) * 64, 512), 1)
+    owner = lax.broadcasted_iota(jnp.int32, (8, 128), 0) == 4 + lax.div(device, 8)
+    small_s[2:4] = narrow[0:2, 0:128]
+    small_s[4:5] = jnp.sum(jnp.where(owner, wide[:, 0:128], 0.0), axis=0, keepdims=True)
+    recv("bz")
     total = bb[2] + rb[4] + rb[5] + rb[6]
-    device = lo * 2 + c
-    narrow = pltpu.roll(total[:, 0:512], lax.rem(512 - device * 16, 512), 1)
-    wide = pltpu.roll(total[:, 0:512], lax.rem(512 - lax.rem(device, 8) * 64, 512), 1)
-    owner = lax.broadcasted_iota(jnp.int32, (8, 128), 0) == 4 + lax.div(device, 8)
-    small_o[0:4] = narrow[0:4, 0:128]
-    small_o[4:5] = jnp.sum(jnp.where(owner, wide[:, 0:128], 0.0), axis=0, keepdims=True)
+    narrow = pltpu.roll(total, lax.rem(128 - lax.rem(device, 8) * 16, 128), 1)
+    for row in range(2):
+        owner = lax.broadcasted_iota(jnp.int32, (16, 128), 0) == row * 4 + lax.div(device, 8)
+        small_s[row : row + 1] = jnp.sum(jnp.where(owner, narrow, 0.0), axis=0, keepdims=True)
     lane = lax.broadcasted_iota(jnp.int32, (1, 128), 1)
-    small_o[5:6] = jnp.where(lane == 0, total[0:1, 512:640], total[1:2, 512:640])
-    small_o[6:8] = jnp.zeros((2, 128), F32)
-
-    layer_out.wait()
-    tg_out.wait()
-    waited |= {("kv", 0), ("kv", 1)} | {("c", F[p]) for p in range(PAIRS - 1)}
-    for key in table:
-        if key not in waited:
-            (cp(*key) if isinstance(key, tuple) else cp(key)).wait_send()
+    small_s[5:6] = jnp.where(lane == 0, total[8:9], total[9:10])
+    small_s[6:8] = jnp.zeros((2, 128), F32)
+    give(small_s, small_o)
+    for one in given:
+        one.wait()
+    for one in sum_batches:
+        if one not in waited:
+            sent(one) if isinstance(one, str) else sent(*one)
 
 
 def results_kernel(*refs):
-    taken, small, given, held, sem = refs[:8], refs[8], refs[9:23], refs[23:31], refs[31]
-    steps = []
-    for i in range(8):
-        there = given[i].at[0] if i < 2 else given[i]
-        steps.append(
-            (
-                pltpu.make_async_copy(taken[i], held[i], sem.at[i]),
-                pltpu.make_async_copy(held[i], there, sem.at[8 + i]),
-            )
-        )
-    for come, _ in steps:
-        come.start()
-    for row, ref in enumerate(given[8:]):
-        ref[...] = small[row, 0 : ref.shape[0]]
-    for come, go in steps:
-        come.wait()
-        go.start()
-    for _, go in steps:
-        go.wait()
+    taken, given, held, ends, sem = refs[:9], refs[9:23], refs[23:32], refs[32:38], refs[38]
+    come = [pltpu.make_async_copy(taken[i], held[i], sem.at[i]) for i in range(9)]
+    go = [
+        pltpu.make_async_copy(held[i], given[i].at[0] if i < 2 else given[i], sem.at[9 + i]) for i in range(8)
+    ] + [pltpu.make_async_copy(ends[i], given[8 + i], sem.at[17 + i]) for i in range(6)]
+    for one in come[8:] + come[:8]:
+        one.start()
+    come[8].wait()
+    for row, ref in enumerate(ends):
+        ref[...] = held[8][row, 0 : ref.shape[0]]
+        go[8 + row].start()
+    for i in (2, 3, 4, 5, 6, 7, 0, 1):
+        come[i].wait()
+        go[i].start()
+    for one in go:
+        one.wait()
 
 
 def scratch():
     v = pltpu.VMEM
     return [
+        v((1, 1024), jnp.int32),
+        pltpu.SMEM((1,), jnp.int32),
+        pltpu.SMEM((2,), F32),
+        *[v((16,), BF)] * 4,
+        v((64,), BF),
+        v((8, 128), F32),
+        v((16, 512), F32),
+        v((16, 512), F32),
+        v((16, 512), F32),
+        v((16, 512), F32),
+        v((16, 2048), F32),
+        v((64, 512), F32),
+        v((8, 128), F32),
         v((1024, 512), BF),
         v((512, 512), BF),
         v((3, 2, 2, 2, 64, 512), BF),
@@ -937,12 +1035,14 @@
         v((2, 3, 64, 384), BF),
         v((2, 3, 64, 384), BF),
         v((128, 512), F32),
-        v((3, 8, 640), F32),
-        v((7, 8, 640), F32),
+        v((3, 16, 128), F32),
+        v((7, 16, 128), F32),
+        v((3, 8, 512), F32),
+        v((7, 8, 512), F32),
         v((32, 128), BF),
-        pltpu.SemaphoreType.DMA((256,)),
-        pltpu.SemaphoreType.DMA((256,)),
-        pltpu.SemaphoreType.DMA((24,)),
+        pltpu.SemaphoreType.DMA((41,)),
+        pltpu.SemaphoreType.DMA((80,)),
+        pltpu.SemaphoreType.DMA((32,)),
     ]
 
 
@@ -989,8 +1089,6 @@
     query_bias, value_bias, output_bias, inner_bias, outer_bias = map(
         block_of, (query_bias, value_bias, output_bias, inner_bias, outer_bias)
     )
-    vmem = pl.BlockSpec(memory_space=pltpu.VMEM)
-    smem = pl.BlockSpec(memory_space=pltpu.SMEM)
     hbm = pl.BlockSpec(memory_space=pl.ANY)
     shape = jax.ShapeDtypeStruct
     outs = pl.pallas_call(
@@ -1006,8 +1104,8 @@
             shape((64, 512), F32),
             shape((8, 128), F32),
         ],
-        in_specs=[hbm, hbm, vmem, smem, smem] + [vmem] * 5 + [hbm] * 6,
-        out_specs=[hbm, hbm] + [vmem] * 7,
+        in_specs=[hbm] * 16,
+        out_specs=[hbm] * 9,
         scratch_shapes=scratch(),
         compiler_params=pltpu.CompilerParams(
             collective_id=0, has_side_effects=True, vmem_limit_bytes=VMEM_BYTES
@@ -1034,9 +1132,11 @@
     outs = pl.pallas_call(
         results_kernel,
         out_shape=[shape((1, 512, 512), BF), shape((1, 512, 512), F32)] + flat,
-        in_specs=[pl.BlockSpec(memory_space=pltpu.HBM)] * 8 + [vmem],
-        out_specs=[hbm] * 8 + [vmem] * 6,
-        scratch_shapes=[pltpu.VMEM(o.shape, o.dtype) for o in outs[:8]] + [pltpu.SemaphoreType.DMA((16,))],
+        in_specs=[pl.BlockSpec(memory_space=pltpu.HBM)] * 9,
+        out_specs=[hbm] * 14,
+        scratch_shapes=[pltpu.VMEM(o.shape, o.dtype) for o in outs]
+        + [pltpu.VMEM(o.shape, o.dtype) for o in flat[6:]]
+        + [pltpu.SemaphoreType.DMA((23,))],
         compiler_params=pltpu.CompilerParams(vmem_limit_bytes=VMEM_BYTES),
     )(*outs)
     layer, token_grads, gq, gk, gv, go, gi, gout, g_query, g_value, g_output, g_outer, g_inner, gate_sums = outs

time: 90.7 us -> 80 us (0.88)
  Pallas kernels: 89 us -> 78.3 us
    pallas_call x1, Pallas kernels: 85.1 us -> 75.4 us  [on_device(): pl.pallas_call(layer_kernel, out_shape=[shape((512, 512), BF), shape((512...]
    pallas_call x1, Pallas kernels: 3.83 us -> 2.91 us  [on_device(): pl.pallas_call(results_kernel, out_shape=[shape((1, 512, 512), BF), shape...]
where the time goes in v3:
time: 80 us; the launch traced here: 79.8 us
  Pallas kernels  78.3 us (98%)
  between operations  1.49 us (2%)
    pallas_call x1, Pallas kernels, on_device(): pl.pallas_call(layer_kernel, out_shape=[shape((512, 512), BF), shape((512...  75.4 us
    pallas_call x1, Pallas kernels, on_device(): pl.pallas_call(results_kernel, out_shape=[shape((1, 512, 512), BF), shape...  2.91 us

profile of v3, /device:TPU:0, one launch (start us, length us, event | category | flops | bytes accessed | tf_op | source)
XLA Modules:
  0.0 79.8 jit_solution(3626987788547011921)
XLA Ops:
  1.3 75.4 %shard_map.263 = (bf16[512,512]{1,0:T(8,128)(2,1)}, f32[512,512]{1,0:T(8,128)}, f32[16,512]{1,0:T(8,128)}, f32[16,512]{1,0:T(8,128)}, f32[16,512]{1,0:T(8,128)},...) custom-call(bf16[512,512]{1,0:T(8,128)(2,1)} %bitcast.2, ...), custom_call_target="tpu_custom_call" | custom-call | tf_op jit(solution)/shard_map/pallas_call | solution.py:1094
  76.7 2.9 %shard_map.264 = (bf16[1,512,512]{2,1,0:T(8,128)(2,1)}, f32[1,512,512]{2,1,0:T(8,128)}, f32[16,512]{1,0:T(8,128)}, f32[16,512]{1,0:T(8,128)}, f32[16,512]{1,0:T(...) custom-call(bf16[512,512]{1,0:T(8,128)(2,1)} %get-tuple-element.37.r, ...), custom_call_target="tpu_custom_call" | custom-call | tf_op jit(solution)/shard_map/pallas_call | solution.py:1132

commit v4 on v3

--- a/solution.py
+++ b/solution.py
@@ -14,7 +14,7 @@
 VMEM_BYTES = 64 * 2**20 - 2**17
 PLAN = {
     "fwd0": ("2q2",),
-    "fwd1": ("2q3", "zf3", "1f1", "3q1",),
+    "fwd1": ("2q3", "1f1", "3q1",),
     "proj1": ("2f0",),
     "fwd2": ("3q2",),
     "fwd3": ("3q3", "1f2",),
@@ -43,7 +43,7 @@
     "fin3": ("FQ2",),
     "tok3": ("EZ", "TQ0", "SQ1", "TO",),
     "last1": ("TQ1", "TQ2",),
-    "start": ("zq2", "1q0", "zq3", "1q1", "zf0", "1q2", "zf1", "1q3", "zf2", "2q0", "3q0", "2q1", "1f0",),
+    "start": ("zq2", "1q0", "zq3", "zf0", "1q1", "zf1", "1q2", "zf2", "1q3", "zf3", "2q0", "3q0", "2q1", "1f0",),
 }
 STEPS = 4
 
@@ -377,6 +377,11 @@
     def inner_block(k):
         return jnp.where(k == 0, 0, k * 16 + 64)
 
+    barrier = pltpu.get_barrier_semaphore()
+    peers = (XP, YP, DP, ZP[1], ZP[2], ZP[3], SB)
+    for dev in peers:
+        pl.semaphore_signal(barrier, inc=1, device_id=dev, device_id_type=MESH)
+
     local = (
         [(tok, xrow.at[pl.ds(0, 512)]), (cot, cotv), (wout, wf.at[0, y, x, c, pl.ds(16, 64)])]
         + [(win.at[:, cols(zs[s])], wf.at[s, y, x, c, pl.ds(0, 16)]) for s in range(STEPS)]
@@ -395,15 +400,11 @@
     needed = [(bias_q, own_q), (bias_v, own_v), (bias_o, own_o), (bias_out, own_out), (bias_in, own_in)]
     needed += [(seg_in, seg), (fill_in, fill), (gates_in, gates)]
     needed = [pltpu.make_async_copy(src, dst, local_sem.at[len(local) + i]) for i, (src, dst) in enumerate(needed)]
-    for one in local[7:11] + needed + local[:7] + local[11:]:
+    for one in needed[:5] + local[7:11] + local[11:] + local[:7] + needed[5:]:
         one.start()
-    barrier = pltpu.get_barrier_semaphore()
-    peers = (XP, YP, DP, ZP[1], ZP[2], ZP[3], SB)
-    for dev in peers:
-        pl.semaphore_signal(barrier, inc=1, device_id=dev, device_id_type=MESH)
 
     biasf[...] = jnp.zeros((8, 128), F32)
-    for one in needed:
+    for one in needed[:5]:
         one.wait()
     for row, ref in enumerate((own_q, own_v, own_o, own_out, own_in)):
         count = ref.shape[0]
@@ -417,7 +418,7 @@
     pl.semaphore_wait(barrier, len(peers))
 
     def send_z(g):
-        for k in (1, 2, 3):
+        for k in (3, 2, 1):
             start("z", g, k)
         if g[0] == "f" and g[1]:
             start("zo", g)
@@ -433,6 +434,9 @@
         recv("z", g)
         for name in neighbours(g):
             start(name, g, 1)
+        if g == ("q", 0):
+            for s in (1, 2, 3):
+                send_early(F[s])
 
     def send_relay(g):
         for name in ("x", "y"):
@@ -464,9 +468,10 @@
         send_early(Q[p])
     for one in local[2:7]:
         one.wait()
-    for s in range(STEPS):
-        send_early(F[s])
-
+    send_early(F[0])
+
+    for one in needed[5:]:
+        one.wait()
     kind = lax.broadcasted_iota(jnp.int32, (16, 512), 0)
     at_own = lax.broadcasted_iota(jnp.int32, (16, 512), 1) + c * 512
     at_sib = lax.broadcasted_iota(jnp.int32, (16, 512), 1) + cc * 512
@@ -918,12 +923,6 @@
     for k in (1, 2, 3):
         go_s[...] += r3w[k - 1].astype(F32)
     give(go_s, go_o)
-    recv("z3q")
-    for p in range(PAIRS):
-        q_last(p)
-    give(gq_s, gq_o)
-    give(gk_s, gk_o)
-    give(gv_s, gv_o)
     recv("ez")
     total = eb[2] + re[4] + re[5] + re[6]
     device = lo * 2 + c
@@ -932,6 +931,12 @@
     owner = lax.broadcasted_iota(jnp.int32, (8, 128), 0) == 4 + lax.div(device, 8)
     small_s[2:4] = narrow[0:2, 0:128]
     small_s[4:5] = jnp.sum(jnp.where(owner, wide[:, 0:128], 0.0), axis=0, keepdims=True)
+    recv("z3q")
+    for p in range(PAIRS):
+        q_last(p)
+    give(gq_s, gq_o)
+    give(gk_s, gk_o)
+    give(gv_s, gv_o)
     recv("bz")
     total = bb[2] + rb[4] + rb[5] + rb[6]
     narrow = pltpu.roll(total, lax.rem(128 - lax.rem(device, 8) * 16, 128), 1)
@@ -942,28 +947,36 @@
     small_s[5:6] = jnp.where(lane == 0, total[8:9], total[9:10])
     small_s[6:8] = jnp.zeros((2, 128), F32)
     give(small_s, small_o)
-    for one in given:
-        one.wait()
     for one in sum_batches:
         if one not in waited:
             sent(one) if isinstance(one, str) else sent(*one)
+    for one in given:
+        one.wait()
 
 
 def results_kernel(*refs):
     taken, given, held, ends, sem = refs[:9], refs[9:23], refs[23:32], refs[32:38], refs[38]
-    come = [pltpu.make_async_copy(taken[i], held[i], sem.at[i]) for i in range(9)]
-    go = [
-        pltpu.make_async_copy(held[i], given[i].at[0] if i < 2 else given[i], sem.at[9 + i]) for i in range(8)
-    ] + [pltpu.make_async_copy(ends[i], given[8 + i], sem.at[17 + i]) for i in range(6)]
-    for one in come[8:] + come[:8]:
+    moves = []
+    for i in (8, 2, 3, 4, 5, 6, 7, 0, 1):
+        rows, parts = taken[i].shape[0], {0: 2, 1: 4}.get(i, 1)
+        for part in range(parts):
+            at = pl.ds(part * rows // parts, rows // parts)
+            there = None if i == 8 else (given[i].at[0] if i < 2 else given[i]).at[at]
+            moves.append((taken[i].at[at], held[i].at[at], there))
+    come = [pltpu.make_async_copy(src, mid, sem.at[n]) for n, (src, mid, _) in enumerate(moves)]
+    for one in come:
         one.start()
-    come[8].wait()
-    for row, ref in enumerate(ends):
-        ref[...] = held[8][row, 0 : ref.shape[0]]
-        go[8 + row].start()
-    for i in (2, 3, 4, 5, 6, 7, 0, 1):
-        come[i].wait()
-        go[i].start()
+    go = []
+    for n, (_, mid, dst) in enumerate(moves):
+        come[n].wait()
+        if n == 0:
+            for row, ref in enumerate(ends):
+                ref[...] = held[8][row, 0 : ref.shape[0]]
+                go.append(pltpu.make_async_copy(ref, given[8 + row], sem.at[len(moves) + row]))
+                go[-1].start()
+        else:
+            go.append(pltpu.make_async_copy(mid, dst, sem.at[len(moves) + 6 + n]))
+            go[-1].start()
     for one in go:
         one.wait()
 
@@ -1136,7 +1149,7 @@
         out_specs=[hbm] * 14,
         scratch_shapes=[pltpu.VMEM(o.shape, o.dtype) for o in outs]
         + [pltpu.VMEM(o.shape, o.dtype) for o in flat[6:]]
-        + [pltpu.SemaphoreType.DMA((23,))],
+        + [pltpu.SemaphoreType.DMA((33,))],
         compiler_params=pltpu.CompilerParams(vmem_limit_bytes=VMEM_BYTES),
     )(*outs)
     layer, token_grads, gq, gk, gv, go, gi, gout, g_query, g_value, g_output, g_outer, g_inner, gate_sums = outs

time: 80 us -> 79 us (0.988)
  Pallas kernels: 78.3 us -> 77.4 us
where the time goes in v4:
time: 79 us; the launch traced here: 78.8 us
  Pallas kernels  77.4 us (98%)
  between operations  1.49 us (2%)
    pallas_call x1, Pallas kernels, on_device(): pl.pallas_call(layer_kernel, out_shape=[shape((512, 512), BF), shape((512...  74.8 us
    pallas_call x1, Pallas kernels, on_device(): pl.pallas_call(results_kernel, out_shape=[shape((1, 512, 512), BF), shape...  2.59 us

profile of v4, /device:TPU:0, one launch (start us, length us, event | category | flops | bytes accessed | tf_op | source)
XLA Modules:
  0.0 78.8 jit_solution(9166995828799515655)
XLA Ops:
  1.3 74.8 %shard_map.263 = (bf16[512,512]{1,0:T(8,128)(2,1)}, f32[512,512]{1,0:T(8,128)}, f32[16,512]{1,0:T(8,128)}, f32[16,512]{1,0:T(8,128)}, f32[16,512]{1,0:T(8,128)},...) custom-call(bf16[512,512]{1,0:T(8,128)(2,1)} %bitcast.2, ...), custom_call_target="tpu_custom_call" | custom-call | tf_op jit(solution)/shard_map/pallas_call | solution.py:1107
  76.1 2.6 %shard_map.264 = (bf16[1,512,512]{2,1,0:T(8,128)(2,1)}, f32[1,512,512]{2,1,0:T(8,128)}, f32[16,512]{1,0:T(8,128)}, f32[16,512]{1,0:T(8,128)}, f32[16,512]{1,0:T(...) custom-call(bf16[512,512]{1,0:T(8,128)(2,1)} %get-tuple-element.37.r, ...), custom_call_target="tpu_custom_call" | custom-call | tf_op jit(solution)/shard_map/pallas_call | solution.py:1145

commit v5 on v4

--- a/solution.py
+++ b/solution.py
@@ -38,8 +38,8 @@
     "bwd6": ("SF3", "TF2",),
     "bwd7": ("FQ1",),
     "fin2": ("SQ0",),
-    "prod7": ("TF3", "EP",),
-    "layer": ("SO",),
+    "prod7": ("TF3",),
+    "layer": ("EP", "SO",),
     "fin3": ("FQ2",),
     "tok3": ("EZ", "TQ0", "SQ1", "TO",),
     "last1": ("TQ1", "TQ2",),
@@ -958,7 +958,7 @@
     taken, given, held, ends, sem = refs[:9], refs[9:23], refs[23:32], refs[32:38], refs[38]
     moves = []
     for i in (8, 2, 3, 4, 5, 6, 7, 0, 1):
-        rows, parts = taken[i].shape[0], {0: 2, 1: 4}.get(i, 1)
+        rows, parts = taken[i].shape[0], {0: 4, 1: 8}.get(i, 1)
         for part in range(parts):
             at = pl.ds(part * rows // parts, rows // parts)
             there = None if i == 8 else (given[i].at[0] if i < 2 else given[i]).at[at]
@@ -1149,7 +1149,7 @@
         out_specs=[hbm] * 14,
         scratch_shapes=[pltpu.VMEM(o.shape, o.dtype) for o in outs]
         + [pltpu.VMEM(o.shape, o.dtype) for o in flat[6:]]
-        + [pltpu.SemaphoreType.DMA((33,))],
+        + [pltpu.SemaphoreType.DMA((45,))],
         compiler_params=pltpu.CompilerParams(vmem_limit_bytes=VMEM_BYTES),
     )(*outs)
     layer, token_grads, gq, gk, gv, go, gi, gout, g_query, g_value, g_output, g_outer, g_inner, gate_sums = outs

time: 79 us -> 79.5 us (level)
  no operation moved by 1% of the time
where the time goes in v5:
time: 79.5 us; the launch traced here: 79.3 us
  Pallas kernels  77.8 us (98%)
  between operations  1.49 us (2%)
    pallas_call x1, Pallas kernels, on_device(): pl.pallas_call(layer_kernel, out_shape=[shape((512, 512), BF), shape((512...  75.2 us
    pallas_call x1, Pallas kernels, on_device(): pl.pallas_call(results_kernel, out_shape=[shape((1, 512, 512), BF), shape...  2.67 us

profile of v5, /device:TPU:0, one launch (start us, length us, event | category | flops | bytes accessed | tf_op | source)
XLA Modules:
  0.0 79.3 jit_solution(4004379344094284961)
XLA Ops:
  1.3 75.2 %shard_map.263 = (bf16[512,512]{1,0:T(8,128)(2,1)}, f32[512,512]{1,0:T(8,128)}, f32[16,512]{1,0:T(8,128)}, f32[16,512]{1,0:T(8,128)}, f32[16,512]{1,0:T(8,128)},...) custom-call(bf16[512,512]{1,0:T(8,128)(2,1)} %bitcast.2, ...), custom_call_target="tpu_custom_call" | custom-call | tf_op jit(solution)/shard_map/pallas_call | solution.py:1107
  76.5 2.7 %shard_map.264 = (bf16[1,512,512]{2,1,0:T(8,128)(2,1)}, f32[1,512,512]{2,1,0:T(8,128)}, f32[16,512]{1,0:T(8,128)}, f32[16,512]{1,0:T(8,128)}, f32[16,512]{1,0:T(...) custom-call(bf16[512,512]{1,0:T(8,128)(2,1)} %get-tuple-element.37.r, ...), custom_call_target="tpu_custom_call" | custom-call | tf_op jit(solution)/shard_map/pallas_call | solution.py:1145
